TPU v7x, 32 devices: a whole 2x2x4 slice. The times are simulated.
32 devices in a mesh: section: 2 (over core), dp: 16 (over z, y, x).
Axes of the slice: x: 2, y: 2, z: 4, core: 2. Of those that a mesh axis runs over, the one named last changes fastest.
Arguments:
- images: bfloat16 [6272, 768], P('dp'), may hold values from -6 to 6
- text: bfloat16 [4096, 768], P('dp'), may hold values from -6 to 6
- enc_mats: bfloat16 [9216, 768], P('dp')
- enc_vecs: bfloat16 [9216], P('dp'), may hold values from -0.8 to 1.3
- dec_mats: bfloat16 [12288, 768], P('dp')
- dec_vecs: bfloat16 [13056], P('dp'), may hold values from -0.8 to 1.3
- tissue: int32 [32, 196], P('dp'), may hold values from 0 to 1, as said below
- text_len: int32 [32], P('dp'), may hold values from 32 to 128, as said below
- enc_cot: bfloat16 [6272, 768], P('dp'), may hold values from -6 to 6
- dec_cot: bfloat16 [4096, 768], P('dp'), may hold values from -6 to 6
Outputs:
- enc_out: bfloat16 [6272, 768], P('dp')
- dec_out: bfloat16 [4096, 768], P('dp')
- image_grad: float32 [6272, 768], P('dp')
- text_grad: float32 [4096, 768], P('dp')
- enc_mats_grad: float32 [9216, 768], P('dp')
- enc_vecs_grad: float32 [9216], P('dp')
- dec_mats_grad: float32 [12288, 768], P('dp')
- dec_vecs_grad: float32 [13056], P('dp')
Inputs may be any that keep to these rules, and one draw needn't show every extreme that they name: `tissue`: each image has between 40 and 196 kept slots, anywhere among its slots; some image has exactly 196 and some exactly 40. `text_len`: some caption has exactly 128 tokens and some exactly 32.
All inputs are finite; a program needn't handle non-finite values.
Results may differ from a plain program's by a relative error of at most 0.025.
The roundings to bfloat16 on the way count: a program that leaves them out, or rounds other values in their place, can miss the bound.
Values may be sent and summed in bfloat16 or wider, within the bound.
A program may use at most 512 MiB of HBM per device.

v0:
```python
import jax
import jax.numpy as jnp
from jax import lax
from jax.sharding import PartitionSpec as P

D = 768
HEAD = 64
FF = 3072
MICRO = 2


def shifted(block, axis, distance):
    devices = range(lax.axis_size(axis))
    route = [(i - distance, i) for i in devices if i - distance in devices]
    return lax.ppermute(block, axis, route)


def layer_norm(inputs, scale_vec, shift_vec):
    centre = inputs - jnp.mean(inputs, axis=-1, keepdims=True)
    spread = jnp.mean(centre * centre, axis=-1, keepdims=True)
    return centre * lax.rsqrt(spread + 1e-06) * scale_vec + shift_vec


def norm_back(inputs, scale_vec, shift_vec, grads):
    _, pullback = jax.vjp(layer_norm, inputs, scale_vec, shift_vec)
    return pullback(grads)


def gelu_back(inner, grads):
    _, pullback = jax.vjp(jax.nn.gelu, inner)
    return pullback(grads)[0]


def part_of(vecs, index):
    return vecs[index * D : (index + 1) * D].astype(jnp.float32)


def split_heads(rows):
    return rows.reshape(rows.shape[0], rows.shape[1], -1, HEAD)


def project(rows, weight):
    return jnp.einsum("bsd,de->bse", rows, weight, preferred_element_type=jnp.float32)


def row_sum(values):
    return jnp.sum(values.astype(jnp.float32), axis=(0, 1))


def attn_scores(queries, key_rows, allowed):
    scores = (
        jnp.einsum(
            "bqhe,bkhe->bhqk",
            split_heads(queries),
            split_heads(key_rows),
            preferred_element_type=jnp.float32,
        )
        * 0.125
    )
    return jnp.where(allowed, scores, -1000000000.0)


def attn_forward(queries, key_rows, value_rows, allowed):
    scores = attn_scores(queries, key_rows, allowed)
    peak = jnp.max(scores, axis=-1, keepdims=True)
    expd = jnp.exp(scores - peak)
    total = jnp.sum(expd, axis=-1, keepdims=True)
    probs = (expd / total).astype(jnp.bfloat16)
    mixed = jnp.einsum(
        "bhqk,bkhe->bqhe", probs, split_heads(value_rows), preferred_element_type=jnp.float32
    )
    return (mixed.reshape(queries.shape).astype(jnp.bfloat16), peak + jnp.log(total))


def attn_backward(queries, key_rows, value_rows, allowed, log_total, grad_mixed):
    scores = attn_scores(queries, key_rows, allowed)
    probs = jnp.exp(scores - log_total)
    grad_heads = split_heads(grad_mixed)
    grad_probs = jnp.einsum(
        "bqhe,bkhe->bhqk", grad_heads, split_heads(value_rows), preferred_element_type=jnp.float32
    )
    grad_scores = probs * (grad_probs - jnp.sum(grad_probs * probs, axis=-1, keepdims=True))
    grad_low = grad_scores.astype(jnp.bfloat16)
    grad_q = (
        jnp.einsum(
            "bhqk,bkhe->bqhe", grad_low, split_heads(key_rows), preferred_element_type=jnp.float32
        )
        * 0.125
    )
    grad_k = (
        jnp.einsum(
            "bhqk,bqhe->bkhe", grad_low, split_heads(queries), preferred_element_type=jnp.float32
        )
        * 0.125
    )
    grad_v = jnp.einsum(
        "bhqk,bqhe->bkhe",
        probs.astype(jnp.bfloat16),
        grad_heads,
        preferred_element_type=jnp.float32,
    )
    return (
        grad_q.reshape(queries.shape),
        grad_k.reshape(key_rows.shape),
        grad_v.reshape(value_rows.shape),
    )


def self_block(inputs, allowed, mats, vecs):
    wqkv = mats[0 : 3 * D].reshape(3, D, D)
    normed = layer_norm(inputs, part_of(vecs, 0), part_of(vecs, 1)).astype(jnp.bfloat16)
    qkv = jnp.einsum("bsd,kde->kbse", normed, wqkv, preferred_element_type=jnp.float32)
    queries = (qkv[0] + part_of(vecs, 2)).astype(jnp.bfloat16)
    key_rows = qkv[1].astype(jnp.bfloat16)
    value_rows = (qkv[2] + part_of(vecs, 3)).astype(jnp.bfloat16)
    mixed, log_total = attn_forward(queries, key_rows, value_rows, allowed)
    after = inputs + project(mixed, mats[3 * D : 4 * D]) + part_of(vecs, 4)
    return (after, (normed, queries, key_rows, value_rows, mixed, log_total))


def self_block_back(inputs, allowed, mats, vecs, saved, grad_after):
    normed, queries, key_rows, value_rows, mixed, log_total = saved
    wqkv = mats[0 : 3 * D].reshape(3, D, D)
    grad_low = grad_after.astype(jnp.bfloat16)
    grad_wout = jnp.einsum("bsd,bse->de", mixed, grad_low, preferred_element_type=jnp.float32)
    grad_mixed = jnp.einsum(
        "bse,de->bsd", grad_low, mats[3 * D : 4 * D], preferred_element_type=jnp.float32
    ).astype(jnp.bfloat16)
    grad_q, grad_k, grad_v = attn_backward(
        queries, key_rows, value_rows, allowed, log_total, grad_mixed
    )
    grad_qkv = jnp.stack([grad_q, grad_k, grad_v]).astype(jnp.bfloat16)
    grad_wqkv = jnp.einsum(
        "bsd,kbse->kde", normed, grad_qkv, preferred_element_type=jnp.float32
    ).reshape(3 * D, D)
    grad_normed = jnp.einsum("kbse,kde->bsd", grad_qkv, wqkv, preferred_element_type=jnp.float32)
    grad_in, grad_gain, grad_shift = norm_back(
        inputs, part_of(vecs, 0), part_of(vecs, 1), grad_normed
    )
    vec_grads = [
        grad_gain,
        grad_shift,
        row_sum(grad_qkv[0]),
        row_sum(grad_qkv[2]),
        row_sum(grad_low),
    ]
    return (grad_after + grad_in, [grad_wqkv, grad_wout], vec_grads)


def cross_block(inputs, image_rows, allowed, mats, vecs):
    normed = layer_norm(inputs, part_of(vecs, 5), part_of(vecs, 6)).astype(jnp.bfloat16)
    queries = (project(normed, mats[4 * D : 5 * D]) + part_of(vecs, 7)).astype(jnp.bfloat16)
    pair = jnp.einsum(
        "bsd,kde->kbse",
        image_rows,
        mats[5 * D : 7 * D].reshape(2, D, D),
        preferred_element_type=jnp.float32,
    )
    key_rows = pair[0].astype(jnp.bfloat16)
    value_rows = (pair[1] + part_of(vecs, 8)).astype(jnp.bfloat16)
    mixed, log_total = attn_forward(queries, key_rows, value_rows, allowed)
    after = inputs + project(mixed, mats[7 * D : 8 * D]) + part_of(vecs, 9)
    return (after, (normed, queries, key_rows, value_rows, mixed, log_total))


def cross_block_back(inputs, image_rows, allowed, mats, vecs, saved, grad_after):
    normed, queries, key_rows, value_rows, mixed, log_total = saved
    grad_low = grad_after.astype(jnp.bfloat16)
    grad_wout = jnp.einsum("bsd,bse->de", mixed, grad_low, preferred_element_type=jnp.float32)
    grad_mixed = jnp.einsum(
        "bse,de->bsd", grad_low, mats[7 * D : 8 * D], preferred_element_type=jnp.float32
    ).astype(jnp.bfloat16)
    grad_q, grad_k, grad_v = attn_backward(
        queries, key_rows, value_rows, allowed, log_total, grad_mixed
    )
    grad_query = grad_q.astype(jnp.bfloat16)
    grad_pair = jnp.stack([grad_k, grad_v]).astype(jnp.bfloat16)
    pair_weight = mats[5 * D : 7 * D].reshape(2, D, D)
    grad_wq = jnp.einsum("bsd,bse->de", normed, grad_query, preferred_element_type=jnp.float32)
    grad_wpair = jnp.einsum(
        "bsd,kbse->kde", image_rows, grad_pair, preferred_element_type=jnp.float32
    ).reshape(2 * D, D)
    grad_image = jnp.einsum(
        "kbse,kde->bsd", grad_pair, pair_weight, preferred_element_type=jnp.float32
    )
    grad_normed = jnp.einsum(
        "bse,de->bsd", grad_query, mats[4 * D : 5 * D], preferred_element_type=jnp.float32
    )
    grad_in, grad_gain, grad_shift = norm_back(
        inputs, part_of(vecs, 5), part_of(vecs, 6), grad_normed
    )
    vec_grads = [
        grad_gain,
        grad_shift,
        row_sum(grad_query),
        row_sum(grad_pair[1]),
        row_sum(grad_low),
    ]
    return (grad_after + grad_in, grad_image, [grad_wq, grad_wpair, grad_wout], vec_grads)


def mlp_block(inputs, w_in_t, w_out, norm_gain, norm_shift, bias_in, bias_out):
    normed = layer_norm(inputs, norm_gain, norm_shift).astype(jnp.bfloat16)
    inner = jnp.einsum("bsd,fd->bsf", normed, w_in_t, preferred_element_type=jnp.float32) + bias_in
    hidden = jax.nn.gelu(inner).astype(jnp.bfloat16)
    result = (
        inputs
        + jnp.einsum("bsf,fd->bsd", hidden, w_out, preferred_element_type=jnp.float32)
        + bias_out
    )
    return (result, (normed, inner, hidden))


def mlp_block_back(inputs, w_in_t, w_out, norm_gain, norm_shift, saved, grad_result):
    normed, inner, hidden = saved
    grad_low = grad_result.astype(jnp.bfloat16)
    grad_w_out = jnp.einsum("bsf,bsd->fd", hidden, grad_low, preferred_element_type=jnp.float32)
    grad_hidden = jnp.einsum("bsd,fd->bsf", grad_low, w_out, preferred_element_type=jnp.float32)
    grad_inner = gelu_back(inner, grad_hidden).astype(jnp.bfloat16)
    grad_w_in = jnp.einsum("bsf,bsd->fd", grad_inner, normed, preferred_element_type=jnp.float32)
    grad_normed = jnp.einsum("bsf,fd->bsd", grad_inner, w_in_t, preferred_element_type=jnp.float32)
    grad_in, grad_gain, grad_shift = norm_back(inputs, norm_gain, norm_shift, grad_normed)
    return (
        grad_result + grad_in,
        [grad_w_in, grad_w_out],
        [grad_gain, grad_shift, row_sum(grad_low), row_sum(grad_inner)],
    )


def encode(image_mb, keep, mats, vecs):
    inputs = image_mb.astype(jnp.float32)
    allowed = (keep > 0.5)[:, None, None, :]
    middle, saved_self = self_block(inputs, allowed, mats, vecs)
    result, saved_mlp = mlp_block(
        middle,
        mats[4 * D : 4 * D + FF],
        mats[4 * D + FF :],
        part_of(vecs, 5),
        part_of(vecs, 6),
        vecs[8 * D : 8 * D + FF].astype(jnp.float32),
        part_of(vecs, 7),
    )
    output = (result * keep[..., None]).astype(jnp.bfloat16)
    return (output, (inputs, allowed, middle, saved_self, saved_mlp))


def encode_back(image_mb, keep, mats, vecs, grad_out):
    _, (inputs, allowed, middle, saved_self, saved_mlp) = encode(image_mb, keep, mats, vecs)
    grad_result = grad_out.astype(jnp.float32) * keep[..., None]
    grad_middle, mats_mlp, vecs_mlp = mlp_block_back(
        middle,
        mats[4 * D : 4 * D + FF],
        mats[4 * D + FF :],
        part_of(vecs, 5),
        part_of(vecs, 6),
        saved_mlp,
        grad_result,
    )
    grad_inputs, mats_self, vecs_self = self_block_back(
        inputs, allowed, mats, vecs, saved_self, grad_middle
    )
    grad_mats = jnp.concatenate(mats_self + mats_mlp, axis=0)
    grad_vecs = jnp.concatenate(vecs_self + vecs_mlp, axis=0)
    return (grad_inputs, grad_mats, grad_vecs)


def decode(text_mb, image_rows, keep, length, mats, vecs):
    inputs = text_mb.astype(jnp.float32)
    positions = jnp.arange(inputs.shape[1])
    causal = (positions[None, :] <= positions[:, None])[None, None] & (
        positions[None, None, None, :] < length[:, None, None, None]
    )
    crossing = (keep > 0.5)[:, None, None, :]
    after_self, saved_self = self_block(inputs, causal, mats, vecs)
    after_cross, saved_cross = cross_block(after_self, image_rows, crossing, mats, vecs)
    result, saved_mlp = mlp_block(
        after_cross,
        mats[8 * D : 8 * D + FF],
        mats[8 * D + FF :],
        part_of(vecs, 10),
        part_of(vecs, 11),
        vecs[13 * D : 13 * D + FF].astype(jnp.float32),
        part_of(vecs, 12),
    )
    return (
        result.astype(jnp.bfloat16),
        (inputs, causal, crossing, after_self, after_cross, saved_self, saved_cross, saved_mlp),
    )


def decode_back(text_mb, image_rows, keep, length, mats, vecs, grad_out):
    _, saved = decode(text_mb, image_rows, keep, length, mats, vecs)
    inputs, causal, crossing, after_self, after_cross, saved_self, saved_cross, saved_mlp = saved
    grad_result = grad_out.astype(jnp.float32)
    grad_cross, mats_mlp, vecs_mlp = mlp_block_back(
        after_cross,
        mats[8 * D : 8 * D + FF],
        mats[8 * D + FF :],
        part_of(vecs, 10),
        part_of(vecs, 11),
        saved_mlp,
        grad_result,
    )
    grad_self, grad_image, mats_cross, vecs_cross = cross_block_back(
        after_self, image_rows, crossing, mats, vecs, saved_cross, grad_cross
    )
    grad_inputs, mats_self, vecs_self = self_block_back(
        inputs, causal, mats, vecs, saved_self, grad_self
    )
    grad_mats = jnp.concatenate(mats_self + mats_cross + mats_mlp, axis=0)
    grad_vecs = jnp.concatenate(vecs_self + vecs_cross + vecs_mlp, axis=0)
    return (grad_inputs, grad_image, grad_mats, grad_vecs)


def body(images, text, enc_mats, enc_vecs, dec_mats, dec_vecs, tissue, text_len, enc_cot, dec_cot):
    first = lax.axis_index("section") == 0
    shards = lax.axis_size("dp")
    img_count, slots = tissue.shape
    batch = img_count // MICRO
    text_rows = text.shape[0] // img_count
    enc_rows, dec_rows = (enc_mats.shape[0], dec_mats.shape[0])
    enc_len, dec_len = (enc_vecs.shape[0], dec_vecs.shape[0])
    keep_all = tissue.astype(jnp.float32).reshape(MICRO, batch, slots)
    image_in = images.reshape(MICRO, batch, slots, D)
    text_in = text.reshape(MICRO, batch, text_rows, D)
    length_in = text_len.reshape(MICRO, batch)
    image_cot = enc_cot.reshape(MICRO, batch, slots, D)
    text_cot = dec_cot.reshape(MICRO, batch, text_rows, D)

    def enc_view(weights):
        mats_part = (
            weights[0].reshape(shards, dec_rows, D)[:, :enc_rows].reshape(shards * enc_rows, D)
        )
        vecs_part = weights[1].reshape(shards, dec_len)[:, :enc_len].reshape(shards * enc_len)
        return (mats_part, vecs_part)

    def dec_view(weights):
        return (weights[0], weights[1])

    def to_padded(grad_mats, grad_vecs):
        mats_part = jnp.pad(
            grad_mats.reshape(shards, enc_rows, D), ((0, 0), (0, dec_rows - enc_rows), (0, 0))
        )
        vecs_part = jnp.pad(grad_vecs.reshape(shards, enc_len), ((0, 0), (0, dec_len - enc_len)))
        return (mats_part.reshape(shards * dec_rows, D), vecs_part.reshape(shards * dec_len))

    mats_pad = jnp.pad(enc_mats, ((0, dec_rows - enc_rows), (0, 0)))
    vecs_pad = jnp.pad(enc_vecs, (0, dec_len - enc_len))
    own_mats = jnp.where(first, mats_pad, dec_mats)
    own_vecs = jnp.where(first, vecs_pad, dec_vecs)
    weights = (
        lax.all_gather(own_mats, "dp", axis=0, tiled=True),
        lax.all_gather(own_vecs, "dp", axis=0, tiled=True),
    )
    zero_image = jnp.zeros((batch, slots, D), jnp.bfloat16)
    zero_text = jnp.zeros((batch, text_rows, D), jnp.bfloat16)
    encoded = [zero_image] * MICRO
    decoded = [zero_text] * MICRO
    for tick in range(MICRO + 1):

        def forward_encoder_work():
            if tick < MICRO:
                mats_part, vecs_part = enc_view(weights)
                return (encode(image_in[tick], keep_all[tick], mats_part, vecs_part)[0], zero_text)
            return (zero_image, zero_text)

        def forward_decoder_work():
            if tick > 0:
                mats_part, vecs_part = dec_view(weights)
                made = decode(
                    text_in[tick - 1],
                    encoded[tick - 1],
                    keep_all[tick - 1],
                    length_in[tick - 1],
                    mats_part,
                    vecs_part,
                )[0]
                return (zero_image, made)
            return (zero_image, zero_text)

        made_image, made_text = lax.cond(first, forward_encoder_work, forward_decoder_work)
        if tick < MICRO:
            arrived = shifted(made_image, "section", 1)
            encoded[tick] = jnp.where(first, made_image, arrived)
        if tick > 0:
            decoded[tick - 1] = made_text
    back_weights = weights
    zero_image_grad = jnp.zeros((batch, slots, D), jnp.float32)
    zero_text_grad = jnp.zeros((batch, text_rows, D), jnp.float32)
    zero_mats = jnp.zeros((shards * dec_rows, D), jnp.float32)
    zero_vecs = jnp.zeros((shards * dec_len,), jnp.float32)
    returned = [zero_image] * MICRO
    image_grads = [zero_image_grad] * MICRO
    text_grads = [zero_text_grad] * MICRO
    total_mats, total_vecs = (zero_mats, zero_vecs)
    for tick in range(MICRO + 1):

        def backward_encoder_work():
            if tick > 0:
                index = MICRO - tick
                mats_part, vecs_part = enc_view(back_weights)
                grad_in, grad_mats, grad_vecs = encode_back(
                    image_in[index], keep_all[index], mats_part, vecs_part, returned[index]
                )
                grad_mats, grad_vecs = to_padded(grad_mats, grad_vecs)
                return (zero_image, zero_text_grad, grad_in, grad_mats, grad_vecs)
            return (zero_image, zero_text_grad, zero_image_grad, zero_mats, zero_vecs)

        def backward_decoder_work():
            if tick < MICRO:
                index = MICRO - 1 - tick
                mats_part, vecs_part = dec_view(back_weights)
                grad_text, grad_image, grad_mats, grad_vecs = decode_back(
                    text_in[index],
                    encoded[index],
                    keep_all[index],
                    length_in[index],
                    mats_part,
                    vecs_part,
                    text_cot[index],
                )
                outgoing = (grad_image + image_cot[index].astype(jnp.float32)).astype(jnp.bfloat16)
                return (outgoing, grad_text, zero_image_grad, grad_mats, grad_vecs)
            return (zero_image, zero_text_grad, zero_image_grad, zero_mats, zero_vecs)

        outgoing, grad_text, grad_in, grad_mats, grad_vecs = lax.cond(
            first, backward_encoder_work, backward_decoder_work
        )
        if tick == 0:
            total_mats, total_vecs = (grad_mats, grad_vecs)
        else:
            total_mats = total_mats + grad_mats
            total_vecs = total_vecs + grad_vecs
        if tick < MICRO:
            returned[MICRO - 1 - tick] = shifted(outgoing, "section", -1)
            text_grads[MICRO - 1 - tick] = grad_text
        if tick > 0:
            image_grads[MICRO - tick] = grad_in
    shard_mats, shard_vecs = (
        lax.psum_scatter(total_mats, "dp", scatter_dimension=0, tiled=True),
        lax.psum_scatter(total_vecs, "dp", scatter_dimension=0, tiled=True),
    )
    image_grad_all = jnp.concatenate(image_grads, axis=0).reshape(-1, D)
    text_grad_all = jnp.concatenate(text_grads, axis=0).reshape(-1, D)
    decoded_all = jnp.concatenate(decoded, axis=0).reshape(-1, D).astype(jnp.float32)
    enc_mats_own = jnp.where(first, shard_mats[:enc_rows], 0.0)
    enc_vecs_own = jnp.where(first, shard_vecs[:enc_len], 0.0)
    dec_mats_own = jnp.where(first, 0.0, shard_mats)
    dec_vecs_own = jnp.where(first, 0.0, shard_vecs)
    image_own = jnp.where(first, image_grad_all, 0.0)
    decoded_own = jnp.where(first, 0.0, decoded_all)
    text_own = jnp.where(first, 0.0, text_grad_all)
    combined = (
        lax.psum(enc_mats_own.astype(jnp.bfloat16), "section").astype(jnp.float32),
        lax.psum(enc_vecs_own.astype(jnp.bfloat16), "section").astype(jnp.float32),
        lax.psum(dec_mats_own.astype(jnp.bfloat16), "section").astype(jnp.float32),
        lax.psum(dec_vecs_own.astype(jnp.bfloat16), "section").astype(jnp.float32),
        lax.psum(image_own.astype(jnp.bfloat16), "section").astype(jnp.float32),
        lax.psum(decoded_own.astype(jnp.bfloat16), "section").astype(jnp.float32),
        lax.psum(text_own.astype(jnp.bfloat16), "section").astype(jnp.float32),
    )
    enc_mats_grad, enc_vecs_grad, dec_mats_grad, dec_vecs_grad, image_grad, dec_full, text_grad = (
        combined
    )
    dec_out = dec_full.astype(jnp.bfloat16)
    enc_out = jnp.concatenate(encoded, axis=0).reshape(-1, D)
    return (
        enc_out,
        dec_out,
        image_grad,
        text_grad,
        enc_mats_grad,
        enc_vecs_grad,
        dec_mats_grad,
        dec_vecs_grad,
    )


def solution(mesh):
    placed = (
        P("dp", None),
        P("dp", None),
        P("dp", None),
        P("dp"),
        P("dp", None),
        P("dp"),
        P("dp", None),
        P("dp"),
        P("dp", None),
        P("dp", None),
    )
    return jax.shard_map(
        body,
        mesh=mesh,
        in_specs=placed,
        out_specs=(
            P("dp", None),
            P("dp", None),
            P("dp", None),
            P("dp", None),
            P("dp", None),
            P("dp"),
            P("dp", None),
            P("dp"),
        ),
        check_vma=False,
    )
```

profile of v0, /device:TPU:0, one launch (start us, length us, event | category | flops | bytes accessed | tf_op | source)
XLA Modules:
  0.0 1354.9 jit_solution(15171786792756182616)
XLA Ops:
  11.6 80.5 %all-reduce.6 = bf16[13056]{0:T(1024)(128)(2,1)S(1)} all-reduce(bf16[13056]{0:T(1024)(128)(2,1)S(1)} %dynamic-update-slice), channel_id=1, replica_groups=mesh['section'=2,'dp'=16] {'dp'}, use_global_device_ids=true, to_apply=%add.6 | all-reduce | flops 13056 | bytes 52224
  92.2 134.9 %all-gather.2.cloned.1.call-done = bf16[12288,768]{1,0:T(8,128)(2,1)} async-done(((bf16[768,768]{1,0:T(8,128)(2,1)}), bf16[12288,768]{1,0:T(8,128)(2,1)}) %all-gather.2.cloned.1.call-update) | async-done | bytes 18874384 | tf_op jit(solution)/shard_map/all_gather | solution.py:352
  227.0 33.4 %conditional.6 = (bf16[1,196,768]{2,1,0:T(8,128)(2,1)S(1)}) conditional(s32[]{:T(128)} %convert_element_type.1807, () %tuple.52, (bf16[2,1,196,768]{3,2,0,1:T(8,128)(2,1)S(1)}, bf16[13056]{0:T(1024)(128)(2,1)S(1)}, bf16[12288,768]{1,0:T(8,128)(2,1)}, f32[2,1,196]{2,1,0:T(1,128)S(1)}) %tuple.64), branch_computations={%region_0.1_spmd, %region_1.8_spmd} | conditional | flops 2906310656 | bytes 124132672 | solution.py:381
  242.1 6.6 slice.752
  254.0 6.5 fusion.52
  263.7 39.7 %conditional.7 = (bf16[1,196,768]{2,1,0:T(8,128)(2,1)}, bf16[1,128,768]{2,1,0:T(8,128)(2,1)S(1)}) conditional(s32[]{:T(128)} %convert_element_type.1807, (bf16[2,1,128,768]{3,2,1,0:T(8,128)(2,1)S(1)}, bf16[13056]{0:T(1024)(128)(2,1)S(1)}, bf16[12288,768]{1,0:T(8,128)(2,1)}, s32[2,1]{0,1:T(1,128)}, bf16[1,196,768]{2,1,0:T(8,128)(2,1)}, ...), branch_computations={%region_8.19_spmd, %region_19.26_spmd} | conditional | flops 2906310656 | bytes 124329288 | solution.py:381
  284.3 6.6 slice.771
  296.2 7.2 fusion.141
  308.5 21.6 %conditional.9 = (bf16[1,196,768]{2,1,0:T(8,128)(2,1)S(1)}, bf16[1,128,768]{2,1,0:T(8,128)(2,1)S(1)}, f32[12288,768]{1,0:T(8,128)}, f32[13056]{0:T(1024)S(1)}) conditional(s32[]{:T(128)} %convert_element_type.1807, (bf16[2,1,128,768]{3,2,1,0:T(8,128)(2,1)S(1)}, bf16[13056]{0:T(1024)(128)(2,1)S(1)}, bf16[12288,768]{1,0:T(8,128)(2,1)}, ...), branch_computations={%region_39.72_spmd, %region_72.73_spmd} | conditional | flops 7546980352 | bytes 291981344 | solution.py:426
  317.6 12.4 broadcast_in_dim.332
  331.4 87.2 %collective-permute-done.2 = bf16[1,196,768]{2,1,0:T(8,128)(2,1)} collective-permute-done((bf16[1,196,768]{2,1,0:T(8,128)(2,1)S(1)}, bf16[1,196,768]{2,1,0:T(8,128)(2,1)}, u32[]{:S(2)}, u32[]{:S(2)}) %collective-permute-start.2) | collective-permute-done | bytes 301088 | tf_op jit(solution)/shard_map/ppermute | solution.py:15
  418.7 124.5 %conditional.10 = (bf16[1,196,768]{2,1,0:T(8,128)(2,1)S(1)}, bf16[1,128,768]{2,1,0:T(8,128)(2,1)S(1)}, bf16[1,196,768]{2,1,0:T(8,128)(2,1)}, f32[12288,768]{1,0:T(8,128)}, f32[13056]{0:T(1024)}) conditional(s32[]{:T(128)} %convert_element_type.1807, (bf16[2,1,128,768]{3,2,1,0:T(8,128)(2,1)S(1)}, bf16[13056]{0:T(1024)(128)(2,1)S(1)}, ...), branch_computations={%region_73.106_spmd, %region_106.127_spmd} | conditional | flops 7820397056 | bytes 337270624 | solution.py:426
  439.2 6.8 slice.780
  449.2 4.9 convert_reduce_fusion.2
  491.8 26.8 %pad_maximum_fusion = f32[9216,768]{1,0:T(8,128)} fusion(f32[3072,768]{1,0:T(8,128)S(1)} %fusion.202, f32[3072,768]{1,0:T(8,128)S(1)} %fusion.261, f32[768,768]{1,0:T(8,128)S(1)} %fusion.234, f32[2304,768]{1,0:T(8,128)} %bitcast.874), kind=kLoop, calls=%fused_computation.172 | loop fusion | flops 21233664 | bytes 56623104 | tf_op jit(solution)/shard_map/cond/branch_1_fun/concatenate | solution.py:262
  518.6 22.2 %pad.16 = f32[16,768,768]{2,1,0:T(8,128)} pad(f32[16,576,768]{2,1,0:T(8,128)} %bitcast.844, f32[]{:T(128)} %constant.268.clone), padding=0_0x0_192x0_0 | pad | bytes 66060292 | tf_op jit(solution)/shard_map/cond/branch_1_fun/jit(_pad)/pad | solution.py:341
  546.8 119.0 %conditional.11 = (bf16[1,196,768]{2,1,0:T(8,128)(2,1)}, f32[12288,768]{1,0:T(8,128)}, f32[13056]{0:T(1024)}) conditional(s32[]{:T(128)} %convert_element_type.1807, () %tuple.57, (bf16[1,196,768]{2,1,0:T(8,128)(2,1)}, f32[2,1,196]{2,1,0:T(1,128)}, bf16[12288,768]{1,0:T(8,128)(2,1)}, bf16[2,1,196,768]{3,2,0,1:T(8,128)(2,1)S(1)}, ...), branch_computations={%region_127.128_spmd, %region_128.149_spmd} | conditional | flops 7820397056 | bytes 336779264 | solution.py:426
  561.7 6.8 slice.798
  571.8 5.2 convert_reduce_fusion.8
  614.6 26.7 %pad_maximum_fusion.4 = f32[9216,768]{1,0:T(8,128)} fusion(f32[3072,768]{1,0:T(8,128)S(1)} %fusion.286, f32[3072,768]{1,0:T(8,128)S(1)} %fusion.345, f32[768,768]{1,0:T(8,128)S(1)} %fusion.318, f32[2304,768]{1,0:T(8,128)} %bitcast.875), kind=kLoop, calls=%fused_computation.314 | loop fusion | flops 21233664 | bytes 56623104 | tf_op jit(solution)/shard_map/cond/branch_1_fun/concatenate | solution.py:262
  641.3 22.3 %pad.18 = f32[16,768,768]{2,1,0:T(8,128)} pad(f32[16,576,768]{2,1,0:T(8,128)} %bitcast.843, f32[]{:T(128)} %constant.282.clone), padding=0_0x0_192x0_0 | pad | bytes 66060292 | tf_op jit(solution)/shard_map/cond/branch_1_fun/jit(_pad)/pad | solution.py:341
  665.8 48.8 %add_add_fusion.14 = f32[12288,768]{1,0:T(8,128)} fusion(f32[12288,768]{1,0:T(8,128)} %get-tuple-element.176, f32[12288,768]{1,0:T(8,128)} %get-tuple-element.174, f32[12288,768]{1,0:T(8,128)} %get-tuple-element.175), kind=kLoop, calls=%fused_computation.1126 | loop fusion | flops 18874368 | bytes 150994944 | tf_op jit(solution)/shard_map/add | solution.py:432
  720.5 534.5 %reduce-scatter.2.cloned.1.call-done = f32[768,768]{1,0:T(8,128)} async-done(((f32[12288,768]{1,0:T(8,128)}), f32[768,768]{1,0:T(8,128)}) %reduce-scatter.2.cloned.1.call-update) | async-done | bytes 2359312 | tf_op jit(solution)/shard_map/reduce_scatter | solution.py:440
  1262.2 75.1 %all-reduce.7 = bf16[13056]{0:T(1024)(128)(2,1)S(1)} all-reduce(f32[13056]{0:T(1024)S(1)} %add_add_fusion.15), channel_id=3, replica_groups=mesh['section'=2,'dp'=16] {'dp'}, use_global_device_ids=true, to_apply=%region_153.154.clone | all-reduce | flops 13056 | bytes 78336
  (478 shorter events, 195.0 us)
Async XLA Ops:
  7.2 219.8 %all-gather.2.cloned.1.call-start = ((), (), s32[]{:S(2)}) async-start(), calls=%async_computation.1 | async-start | bytes 20054016 | tf_op jit(solution)/shard_map/all_gather | solution.py:352
  9.8 1245.2 %reduce-scatter.2.cloned.1.call-start = ((), (), s32[]{:S(2)}) async-start(), calls=%async_computation.2 | async-start | bytes 40108032 | tf_op jit(solution)/shard_map/reduce_scatter | solution.py:440
  9.9 408.7 %copy-start.164 = (f32[2,1,196]{2,1,0:T(1,128)}, f32[2,1,196]{2,1,0:T(1,128)S(1)}, u32[]{:S(2)}) copy-start(f32[2,1,196]{2,1,0:T(1,128)S(1)} %reshape.5018) | copy-start | bytes 4708
  227.0 36.7 %copy-start = (bf16[256,768]{1,0:T(8,128)(2,1)S(1)}, bf16[256,768]{1,0:T(8,128)(2,1)}, u32[]{:S(2)}) copy-start(bf16[256,768]{1,0:T(8,128)(2,1)} %param.23) | copy-start | bytes 1179652
  260.5 2.5 collective-permute-start
  303.4 3.3 collective-permute-start.1
  330.1 88.6 %copy-start.109 = (bf16[1,128,768]{2,1,0:T(8,128)(2,1)}, bf16[1,128,768]{2,1,0:T(8,128)(2,1)S(1)}, u32[]{:S(2)}) copy-start(bf16[1,128,768]{2,1,0:T(8,128)(2,1)S(1)} %get-tuple-element.173) | copy-start | bytes 589828
  330.1 88.6 %copy-start.142 = (f32[13056]{0:T(1024)}, f32[13056]{0:T(1024)S(1)}, u32[]{:S(2)}) copy-start(f32[13056]{0:T(1024)S(1)} %get-tuple-element.177) | copy-start | bytes 156676
  330.1 88.5 %collective-permute-start.2 = (bf16[1,196,768]{2,1,0:T(8,128)(2,1)S(1)}, bf16[1,196,768]{2,1,0:T(8,128)(2,1)}, u32[]{:S(2)}, u32[]{:S(2)}) collective-permute-start(bf16[1,196,768]{2,1,0:T(8,128)(2,1)S(1)} %get-tuple-element.168), channel_id=1, source_target_pairs={{16,0},{17,1},{18,2},{19,3},{20,4},{21,5},{22,6},{23,7},{24,8},{25... | collective-permute-start | bytes 903176 | tf_op jit(solution)/shard_map/ppermute | solution.py:15
  439.2 6.8 copy-start.133
  446.5 9.5 copy-start.38
  446.6 9.5 copy-start.173
  446.8 9.2 copy-start.193
  518.6 22.3 %copy-start.33 = (f32[196,768]{1,0:T(8,128)S(1)}, f32[196,768]{1,0:T(8,128)}, u32[]{:S(2)}) copy-start(f32[196,768]{1,0:T(8,128)} %copy-done.32) | copy-start | bytes 1806340 | tf_op jit(solution)/shard_map/cond
  518.6 22.3 %copy-start.192 = (f32[196]{0:T(256)S(1)}, f32[196]{0:T(256)}, u32[]{:S(2)}) copy-start(f32[196]{0:T(256)} %copy-done.191) | copy-start | bytes 2356 | tf_op jit(solution)/shard_map/cond
  543.2 3.6 collective-permute-start.3
  561.7 6.8 copy-start.135
  561.7 6.8 copy-start.213
  569.1 9.8 copy-start.40
  569.1 9.8 copy-start.175
  569.3 9.5 copy-start.195
  641.3 22.3 %copy-start.31 = (f32[196,768]{1,0:T(8,128)S(1)}, f32[196,768]{1,0:T(8,128)}, u32[]{:S(2)}) copy-start(f32[196,768]{1,0:T(8,128)} %copy-done.30) | copy-start | bytes 1806340 | tf_op jit(solution)/shard_map/cond
  641.3 22.3 %copy-start.190 = (f32[196]{0:T(256)S(1)}, f32[196]{0:T(256)}, u32[]{:S(2)}) copy-start(f32[196]{0:T(256)} %copy-done.189) | copy-start | bytes 2356 | tf_op jit(solution)/shard_map/cond
  714.7 626.3 %all-reduce.12.cloned.1.call-start = ((), (), s32[]{:S(2)}) async-start(), calls=%async_computation.3 | async-start | bytes 6905856 | tf_op jit(solution)/shard_map/psum | solution.py:459
  (102 other events, 320.4 us)
Sparse Core Ops, SparseCore 0:
  11.4 215.5 all-gather.1
  714.8 540.0 reduce-scatter.1
  1258.8 24.5 all-reduce.11
where the time goes:
time: 1360 us; the launch traced here: 1350 us
  waiting for transfers between devices  760 us (56%)
  blocking collectives  158 us (12%)
  local copies, waits for them, and re-layouts  154 us (11%)
  other arithmetic  141 us (10%)
  matrix products  98.4 us (7%)
  loops' own time  22.5 us (2%)
  between operations  15.6 us (1%)
    reduce_scatter x1, waiting for transfers between devices, body(): lax.psum_scatter(total_mats, 'dp', scatter_dimension=0, tiled=True)  534 us
    unnamed x2, blocking collectives  156 us
    all_gather x1, waiting for transfers between devices, body(): lax.all_gather(own_mats, 'dp', axis=0, tiled=True)  135 us
    ppermute x4, waiting for transfers between devices, shifted(): return lax.ppermute(block, axis, route)  90.8 us
    concatenate x2, other arithmetic, encode_back(): grad_mats = jnp.concatenate(mats_self + mats_mlp, axis=0)  53.5 us
    add x1, other arithmetic, body(): total_mats = total_mats + grad_mats  48.8 us
    pad x2, local copies, waits for them, and re-layouts, to_padded(): jnp.pad(grad_mats.reshape(shards, enc_rows, D), ((0, 0), (0, dec_rows - e...  44.5 us
  transfers between devices with their start and end apart: 7, of which 5 were waited for; matrix products, arithmetic and copies ran while one was open for 1% of the time, Pallas kernels for 0%

commit v1 on v0

--- a/solution.py
+++ b/solution.py
@@ -1,6 +1,10 @@
+import functools
+
 import jax
 import jax.numpy as jnp
 from jax import lax
+from jax.experimental import pallas as pl
+from jax.experimental.pallas import tpu as pltpu
 from jax.sharding import PartitionSpec as P
 
 D = 768
@@ -244,8 +248,8 @@
     return (output, (inputs, allowed, middle, saved_self, saved_mlp))
 
 
-def encode_back(image_mb, keep, mats, vecs, grad_out):
-    _, (inputs, allowed, middle, saved_self, saved_mlp) = encode(image_mb, keep, mats, vecs)
+def encode_back(saved, keep, mats, vecs, grad_out):
+    inputs, allowed, middle, saved_self, saved_mlp = saved
     grad_result = grad_out.astype(jnp.float32) * keep[..., None]
     grad_middle, mats_mlp, vecs_mlp = mlp_block_back(
         middle,
@@ -259,9 +263,7 @@
     grad_inputs, mats_self, vecs_self = self_block_back(
         inputs, allowed, mats, vecs, saved_self, grad_middle
     )
-    grad_mats = jnp.concatenate(mats_self + mats_mlp, axis=0)
-    grad_vecs = jnp.concatenate(vecs_self + vecs_mlp, axis=0)
-    return (grad_inputs, grad_mats, grad_vecs)
+    return (grad_inputs, mats_self + mats_mlp, vecs_self + vecs_mlp)
 
 
 def decode(text_mb, image_rows, keep, length, mats, vecs):
@@ -284,13 +286,32 @@
     )
     return (
         result.astype(jnp.bfloat16),
-        (inputs, causal, crossing, after_self, after_cross, saved_self, saved_cross, saved_mlp),
-    )
-
-
-def decode_back(text_mb, image_rows, keep, length, mats, vecs, grad_out):
-    _, saved = decode(text_mb, image_rows, keep, length, mats, vecs)
-    inputs, causal, crossing, after_self, after_cross, saved_self, saved_cross, saved_mlp = saved
+        (
+            inputs,
+            image_rows,
+            causal,
+            crossing,
+            after_self,
+            after_cross,
+            saved_self,
+            saved_cross,
+            saved_mlp,
+        ),
+    )
+
+
+def decode_back(saved, mats, vecs, grad_out):
+    (
+        inputs,
+        image_rows,
+        causal,
+        crossing,
+        after_self,
+        after_cross,
+        saved_self,
+        saved_cross,
+        saved_mlp,
+    ) = saved
     grad_result = grad_out.astype(jnp.float32)
     grad_cross, mats_mlp, vecs_mlp = mlp_block_back(
         after_cross,
@@ -307,12 +328,15 @@
     grad_inputs, mats_self, vecs_self = self_block_back(
         inputs, causal, mats, vecs, saved_self, grad_self
     )
-    grad_mats = jnp.concatenate(mats_self + mats_cross + mats_mlp, axis=0)
-    grad_vecs = jnp.concatenate(vecs_self + vecs_cross + vecs_mlp, axis=0)
-    return (grad_inputs, grad_image, grad_mats, grad_vecs)
-
-
-def body(images, text, enc_mats, enc_vecs, dec_mats, dec_vecs, tissue, text_len, enc_cot, dec_cot):
+    return (
+        grad_inputs,
+        grad_image,
+        mats_self + mats_cross + mats_mlp,
+        vecs_self + vecs_cross + vecs_mlp,
+    )
+
+
+def body_plain(images, text, enc_mats, enc_vecs, dec_mats, dec_vecs, tissue, text_len, enc_cot, dec_cot):
     first = lax.axis_index("section") == 0
     shards = lax.axis_size("dp")
     img_count, slots = tissue.shape
@@ -399,10 +423,13 @@
             if tick > 0:
                 index = MICRO - tick
                 mats_part, vecs_part = enc_view(back_weights)
+                _, saved = encode(image_in[index], keep_all[index], mats_part, vecs_part)
                 grad_in, grad_mats, grad_vecs = encode_back(
-                    image_in[index], keep_all[index], mats_part, vecs_part, returned[index]
+                    saved, keep_all[index], mats_part, vecs_part, returned[index]
                 )
-                grad_mats, grad_vecs = to_padded(grad_mats, grad_vecs)
+                grad_mats, grad_vecs = to_padded(
+                    jnp.concatenate(grad_mats, axis=0), jnp.concatenate(grad_vecs, axis=0)
+                )
                 return (zero_image, zero_text_grad, grad_in, grad_mats, grad_vecs)
             return (zero_image, zero_text_grad, zero_image_grad, zero_mats, zero_vecs)
 
@@ -410,15 +437,19 @@
             if tick < MICRO:
                 index = MICRO - 1 - tick
                 mats_part, vecs_part = dec_view(back_weights)
-                grad_text, grad_image, grad_mats, grad_vecs = decode_back(
+                _, saved = decode(
                     text_in[index],
                     encoded[index],
                     keep_all[index],
                     length_in[index],
                     mats_part,
                     vecs_part,
-                    text_cot[index],
                 )
+                grad_text, grad_image, grad_mats, grad_vecs = decode_back(
+                    saved, mats_part, vecs_part, text_cot[index]
+                )
+                grad_mats = jnp.concatenate(grad_mats, axis=0)
+                grad_vecs = jnp.concatenate(grad_vecs, axis=0)
                 outgoing = (grad_image + image_cot[index].astype(jnp.float32)).astype(jnp.bfloat16)
                 return (outgoing, grad_text, zero_image_grad, grad_mats, grad_vecs)
             return (zero_image, zero_text_grad, zero_image_grad, zero_mats, zero_vecs)
@@ -476,6 +507,1650 @@
     )
 
 
+MESH = pl.DeviceIdType.MESH
+TILE = 16
+ADD_ROWS = 32
+
+
+def grid_of(shards):
+    return (shards // 4, 2, 2)
+
+
+def split_rows(rows, late):
+    part = int(rows * late / 2) // TILE * TILE
+    first = (rows - 2 * part) // 2 // TILE * TILE
+    sizes = (first, rows - 2 * part - first, part, part)
+    starts = (0, first, rows - 2 * part, rows - part)
+    return tuple(zip(starts, sizes))
+
+
+class Place:
+    def __init__(self, depth):
+        self.section = lax.axis_index("section")
+        self.me = lax.axis_index("dp")
+        self.depth = depth
+        self.z = lax.div(self.me, 4)
+        self.y = lax.rem(lax.div(self.me, 2), 2)
+        self.x = lax.rem(self.me, 2)
+
+    def shard(self, z, y, x):
+        return (z * 2 + y) * 2 + x
+
+    def pair(self, first_x, z, first, second):
+        return self.shard(z, second, first) if first_x else self.shard(z, first, second)
+
+    def own(self, first_x):
+        return (self.x, self.y) if first_x else (self.y, self.x)
+
+
+class Copies:
+    def __init__(self, place, waiting=False):
+        self.place = place
+        self.waiting = waiting
+
+    def start(self, cond, src, dst, send_sem, recv_sem, dp, section=None):
+        section = self.place.section if section is None else section
+
+        def act():
+            copy = pltpu.make_async_remote_copy(
+                src_ref=src,
+                dst_ref=dst,
+                send_sem=send_sem,
+                recv_sem=recv_sem,
+                device_id=(section, dp),
+                device_id_type=MESH,
+            )
+            if self.waiting:
+                copy.wait_send()
+            else:
+                copy.start()
+
+        if cond is None:
+            act()
+        else:
+            pl.when(cond)(act)
+
+    def arrived(self, dst, send_sem, recv_sem):
+        if self.waiting:
+            return
+        pltpu.make_async_remote_copy(
+            src_ref=dst,
+            dst_ref=dst,
+            send_sem=send_sem,
+            recv_sem=recv_sem,
+            device_id=(self.place.section, self.place.me),
+            device_id_type=MESH,
+        ).wait_recv()
+
+
+def guarded(cond, step, *args):
+    if cond is None:
+        step(*args)
+    else:
+        pl.when(cond)(functools.partial(step, *args))
+
+
+def greet(place, shards, both):
+    barrier = pltpu.get_barrier_semaphore()
+    for step in range(1, shards):
+        pl.semaphore_signal(
+            barrier,
+            inc=1,
+            device_id=(place.section, lax.rem(place.me + step, shards)),
+            device_id_type=MESH,
+        )
+    if both:
+        pl.semaphore_signal(
+            barrier, inc=1, device_id=(1 - place.section, place.me), device_id_type=MESH
+        )
+    pl.semaphore_wait(barrier, shards - 1 + int(both))
+
+
+class Gather:
+    def __init__(self, copies, place, depth, rows, cuts, w, send_sems, recv_sems, gate):
+        self.copies = copies
+        self.gate = gate
+        self.place = place
+        self.depth = depth
+        self.rows = rows
+        self.cuts = cuts
+        self.w = w
+        self.send_sems = send_sems
+        self.recv_sems = recv_sems
+        self.late = (2, 3) if cuts[2][1] else ()
+
+    def piece(self, cls, shard):
+        start, size = self.cuts[cls]
+        return self.w.at[pl.ds(pl.multiple_of(shard * self.rows + start, TILE), size)]
+
+    def send(self, cls, shard, way, dp):
+        piece = self.piece(cls, shard)
+        self.copies.start(
+            None, piece, piece, self.send_sems.at[cls, shard, way], self.recv_sems.at[cls, shard], dp
+        )
+
+    def arrived(self, cls, shard):
+        self.copies.arrived(
+            self.piece(cls, shard), self.send_sems.at[cls, shard, 0], self.recv_sems.at[cls, shard]
+        )
+
+    def along(self, plane, distance, act):
+        z, last = self.place.z, self.depth - 1
+        if distance == 0:
+            pl.when(z == plane)(lambda: act(plane, plane < last, plane > 0))
+            return
+        if plane + distance <= last:
+            pl.when(z == plane + distance)(
+                lambda: act(plane + distance, plane + distance < last, False)
+            )
+        if plane - distance >= 0:
+            pl.when(z == plane - distance)(
+                lambda: act(plane - distance, False, plane - distance > 0)
+            )
+
+    def L(self, plane, distance):
+        place = self.place
+
+        def act(at, up, down):
+            shard = place.shard(plane, place.y, place.x)
+            for cls in (0, 1):
+                a, b = place.own(cls == 0)
+                if distance:
+                    self.arrived(cls, shard)
+                if up:
+                    self.send(cls, shard, 0, place.me + 4)
+                if down:
+                    self.send(cls, shard, 1, place.me - 4)
+                self.send(cls, shard, 2, place.pair(cls == 0, at, 1 - a, b))
+
+        self.along(plane, distance, act)
+
+    def G(self, plane, distance):
+        place = self.place
+
+        def act(at, up, down):
+            for cls in (0, 1):
+                a, b = place.own(cls == 0)
+                other = place.pair(cls == 0, plane, 1 - a, b)
+                self.arrived(cls, other)
+                to = place.pair(cls == 0, at, a, 1 - b)
+                self.send(cls, place.shard(plane, place.y, place.x), 3, to)
+                self.send(cls, other, 3, to)
+
+        self.along(plane, distance, act)
+
+    def H(self, plane):
+        place = self.place
+        for cls in (0, 1):
+            a, b = place.own(cls == 0)
+            self.arrived(cls, place.pair(cls == 0, plane, a, 1 - b))
+            self.arrived(cls, place.pair(cls == 0, plane, 1 - a, 1 - b))
+
+    def X(self):
+        if not self.copies.waiting:
+            self.gate()
+
+    def M(self):
+        place = self.place
+        for cls in self.late:
+            a, b = place.own(cls == 2)
+            self.send(cls, place.me, 2, place.pair(cls == 2, place.z, 1 - a, b))
+
+    def N(self):
+        place = self.place
+        for cls in self.late:
+            a, b = place.own(cls == 2)
+            other = place.pair(cls == 2, place.z, 1 - a, b)
+            self.arrived(cls, other)
+            to = place.pair(cls == 2, place.z, a, 1 - b)
+            self.send(cls, place.me, 3, to)
+            self.send(cls, other, 3, to)
+
+    def T(self, plane, distance):
+        place = self.place
+
+        def act(at, up, down):
+            for cls in self.late:
+                a, b = place.own(cls == 2)
+                if distance == 0:
+                    self.arrived(cls, place.pair(cls == 2, plane, a, 1 - b))
+                    self.arrived(cls, place.pair(cls == 2, plane, 1 - a, 1 - b))
+                for index in range(4):
+                    shard = plane * 4 + index
+                    if distance:
+                        self.arrived(cls, shard)
+                    if up:
+                        self.send(cls, shard, 0, place.me + 4)
+                    if down:
+                        self.send(cls, shard, 1, place.me - 4)
+
+        self.along(plane, distance, act)
+
+
+def add_rows(total, total_start, part, part_start, size):
+    step = next(n for n in (64, 48, 32, TILE) if size % n == 0)
+
+    @pl.loop(0, size // step)
+    def _(index):
+        at = pl.ds(pl.multiple_of(total_start + index * step, TILE), step)
+        of = pl.ds(pl.multiple_of(part_start + index * step, TILE), step)
+        total[at] = total[at] + part[of]
+
+
+class Scatter:
+    def __init__(self, copies, place, depth, rows, cuts, g, land, send_sems, recv_sems, done):
+        self.copies = copies
+        self.done = done
+        self.place = place
+        self.depth = depth
+        self.rows = rows
+        self.cuts = cuts
+        self.g = g
+        self.land = land
+        self.send_sems = send_sems
+        self.recv_sems = recv_sems
+        self.late = (2, 3) if cuts[2][1] else ()
+        self.early_slots = 4 * depth + 1
+        self.late_slots = 4 * depth + 7
+
+    @staticmethod
+    def land_rows(depth, cuts):
+        early = (4 * depth + 1) * (cuts[0][1] + cuts[1][1])
+        return early + (4 * depth + 7) * (cuts[2][1] + cuts[3][1])
+
+    def start_of(self, cls, shard):
+        return pl.multiple_of(shard * self.rows + self.cuts[cls][0], TILE)
+
+    def slot_start(self, cls, slot):
+        base = 0
+        for other in range(cls):
+            base += (self.early_slots if other < 2 else self.late_slots) * self.cuts[other][1]
+        return base + slot * self.cuts[cls][1]
+
+    def slot_ref(self, cls, slot):
+        return self.land.at[pl.ds(self.slot_start(cls, slot), self.cuts[cls][1])]
+
+    def send(self, cls, shard, slot, dp):
+        self.copies.start(
+            None,
+            self.g.at[pl.ds(self.start_of(cls, shard), self.cuts[cls][1])],
+            self.slot_ref(cls, slot),
+            self.send_sems.at[cls, slot],
+            self.recv_sems.at[cls, slot],
+            dp,
+        )
+
+    def take(self, cls, shard, slot):
+        if self.copies.waiting:
+            return
+        self.copies.arrived(
+            self.slot_ref(cls, slot), self.send_sems.at[cls, slot], self.recv_sems.at[cls, slot]
+        )
+        add_rows(
+            self.g,
+            self.start_of(cls, shard),
+            self.land,
+            self.slot_start(cls, slot),
+            self.cuts[cls][1],
+        )
+
+    def A(self, plane):
+        place = self.place
+        for cls in (0, 1):
+            first_x = cls == 0
+            a, b = place.own(first_x)
+            to = place.pair(first_x, place.z, 1 - a, b)
+            self.send(cls, place.pair(first_x, plane, 1 - a, 1 - b), plane * 3, to)
+            self.send(cls, place.pair(first_x, plane, 1 - a, b), plane * 3 + 1, to)
+
+    def B(self, plane):
+        place = self.place
+        for cls in (0, 1):
+            first_x = cls == 0
+            a, b = place.own(first_x)
+            away = place.pair(first_x, plane, a, 1 - b)
+            self.take(cls, away, plane * 3)
+            self.send(cls, away, plane * 3 + 2, place.pair(first_x, place.z, a, 1 - b))
+        for cls in (0, 1):
+            first_x = cls == 0
+            a, b = place.own(first_x)
+            self.take(cls, place.pair(first_x, plane, a, b), plane * 3 + 1)
+
+    def P(self, plane):
+        place = self.place
+        for cls in (0, 1):
+            self.take(cls, place.shard(plane, place.y, place.x), plane * 3 + 2)
+
+    def hop(self, plane, number, act):
+        z = self.place.z
+        low, high = number - 1, self.depth - number
+        if low < plane:
+            pl.when(z == low)(lambda: act(1, low + 1 == plane))
+        if high > plane:
+            pl.when(z == high)(lambda: act(-1, high - 1 == plane))
+
+    def Z(self, plane, number):
+        place = self.place
+        slot = 3 * self.depth + plane
+
+        def act(way, ends):
+            shard = place.shard(plane, place.y, place.x)
+            for cls in (0, 1):
+                if number > 1:
+                    self.take(cls, shard, slot)
+                to = 4 * self.depth if ends and way < 0 else slot
+                self.send(cls, shard, to, place.me + 4 * way)
+
+        self.hop(plane, number, act)
+
+    def E(self, plane):
+        place = self.place
+
+        @pl.when(place.z == plane)
+        def _():
+            shard = place.shard(plane, place.y, place.x)
+            for cls in (0, 1):
+                if plane > 0:
+                    self.take(cls, shard, 3 * self.depth + plane)
+                if plane < self.depth - 1:
+                    self.take(cls, shard, 4 * self.depth)
+                if not self.copies.waiting:
+                    self.done(cls)
+
+    def Q(self, plane, number):
+        place = self.place
+
+        def act(way, ends):
+            for cls in self.late:
+                for index in range(4):
+                    slot = plane * 4 + index
+                    if number > 1:
+                        self.take(cls, slot, slot)
+                    to = 4 * self.depth + index if ends and way < 0 else slot
+                    self.send(cls, slot, to, place.me + 4 * way)
+
+        self.hop(plane, number, act)
+
+    def R(self, plane):
+        place = self.place
+        base = 4 * self.depth + 4
+
+        @pl.when(place.z == plane)
+        def _():
+            for cls in self.late:
+                for index in range(4):
+                    slot = plane * 4 + index
+                    if plane > 0:
+                        self.take(cls, slot, slot)
+                    if plane < self.depth - 1:
+                        self.take(cls, slot, 4 * self.depth + index)
+                first_x = cls == 2
+                a, b = place.own(first_x)
+                to = place.pair(first_x, plane, 1 - a, b)
+                self.send(cls, place.pair(first_x, plane, 1 - a, 1 - b), base, to)
+                self.send(cls, place.pair(first_x, plane, 1 - a, b), base + 1, to)
+
+    def S(self, plane):
+        place = self.place
+        base = 4 * self.depth + 4
+
+        @pl.when(place.z == plane)
+        def _():
+            for cls in self.late:
+                first_x = cls == 2
+                a, b = place.own(first_x)
+                away = place.pair(first_x, plane, a, 1 - b)
+                self.take(cls, away, base)
+                self.send(cls, away, base + 2, place.pair(first_x, plane, a, 1 - b))
+            for cls in self.late:
+                a, b = place.own(cls == 2)
+                self.take(cls, place.pair(cls == 2, plane, a, b), base + 1)
+            for cls in self.late:
+                self.take(cls, place.me, base + 2)
+                if not self.copies.waiting:
+                    self.done(cls)
+
+
+STEPS = "CLGHMNTABPZEQRSX"
+
+
+LAG = 14
+
+
+class Plan:
+    def __init__(self, steps, copies, sent, stages):
+        self.steps = steps
+        self.copies = copies
+        self.sent = sent
+        self.stages = stages
+        self.open = []
+
+    @staticmethod
+    def act(copies, step):
+        kind, plane, hop = step // 100, step // 10 % 10, step % 10
+        act = getattr(copies, STEPS[kind])
+        if STEPS[kind] in "LGTZQ":
+            act(plane, hop)
+        elif STEPS[kind] in "MNX":
+            act()
+        else:
+            act(plane)
+
+    def run(self):
+        for step in self.steps:
+            if step < 100:
+                self.stages[step]()
+                continue
+            self.act(self.copies, step)
+            self.open.append(step)
+            if len(self.open) > LAG:
+                self.act(self.sent, self.open.pop(0))
+
+    def flush(self):
+        for step in self.open:
+            self.act(self.sent, step)
+        self.open.clear()
+
+
+BLOCK = 256
+LINES = 32
+NORM_ROWS = 64
+UNROLL = 3
+ATTEND_UNROLL = 2
+PAIRS = D // 128
+VEC_UNIT = 48
+VEC_ROWS = 32
+F32 = jnp.float32
+BF16 = jnp.bfloat16
+
+
+def dot_nn(left, right):
+    return lax.dot_general(left, right, (((1,), (0,)), ((), ())), preferred_element_type=F32)
+
+
+def dot_nt(left, right):
+    return lax.dot_general(left, right, (((1,), (1,)), ((), ())), preferred_element_type=F32)
+
+
+def dot_tn(left, right):
+    return lax.dot_general(left, right, (((0,), (0,)), ((), ())), preferred_element_type=F32)
+
+
+def chunk(start, size=BLOCK):
+    if isinstance(start, int):
+        return pl.ds(start, size)
+    return pl.ds(pl.multiple_of(start, 128 if size % 128 == 0 else TILE), size)
+
+
+def iota(shape, dim):
+    return lax.broadcasted_iota(jnp.int32, shape, dim)
+
+
+def unit_of(column):
+    return lax.shift_right_logical(column * 1366, 16)
+
+
+def unit_spread():
+    column = iota((128, D), 1)
+    return (column - VEC_UNIT * unit_of(column) == iota((128, D), 0)).astype(BF16)
+
+
+def vec_gathered(tiles, per):
+    shards = tiles.shape[0]
+    count = shards * VEC_ROWS
+    spread = dot_nn(tiles[...].reshape(count, 128), unit_spread())
+    row = iota((count, D), 0)
+    inner = row & (VEC_ROWS - 1)
+    unit = lax.shift_right_logical(row, 5) * per + inner
+    mask = ((unit & 15) == unit_of(iota((count, D), 1))) & (inner < per)
+    spread = jnp.where(mask, spread, 0.0).astype(BF16)
+    row = iota((VEC_ROWS, count), 1)
+    inner = row & (VEC_ROWS - 1)
+    unit = lax.shift_right_logical(row, 5) * per + inner
+    pick = (lax.shift_right_logical(unit, 4) == iota((VEC_ROWS, count), 0)) & (inner < per)
+    return dot_nn(pick.astype(F32).astype(BF16), spread)
+
+
+def exact_dot(pick, values, dot):
+    high = values.astype(BF16)
+    rest = values - high.astype(F32)
+    middle = rest.astype(BF16)
+    low = (rest - middle.astype(F32)).astype(BF16)
+    return dot(pick, high) + dot(pick, middle) + dot(pick, low)
+
+
+def vec_shard(rows, me, per):
+    unit = me * per + iota((VEC_ROWS, VEC_ROWS), 0)
+    pick = (lax.shift_right_logical(unit, 4) == iota((VEC_ROWS, VEC_ROWS), 1)).astype(F32)
+    lines = exact_dot(pick.astype(BF16), rows, dot_nn)
+    unit = me * per + iota((VEC_ROWS, D), 0)
+    mask = (unit & 15) == unit_of(iota((VEC_ROWS, D), 1))
+    lines = jnp.where(mask, lines, 0.0)
+    spread = unit_spread()
+    return exact_dot(spread, lines, lambda pick, part: dot_nt(part, pick))
+
+
+def in_line(tile):
+    group = 8 * VEC_UNIT
+    column = iota((128, group), 1)
+    pick = (column - VEC_UNIT * unit_of(column) == iota((128, group), 0)).astype(F32)
+    spread = exact_dot(pick.astype(BF16), tile, lambda pick, part: dot_nn(part, pick))
+    mask = (iota((VEC_ROWS, group), 0) & 7) == unit_of(iota((VEC_ROWS, group), 1))
+    spread = jnp.where(mask, spread, 0.0)
+    gather = lax.shift_right_logical(iota((8, VEC_ROWS), 1), 3) == iota((8, VEC_ROWS), 0)
+    lines = exact_dot(gather.astype(F32).astype(BF16), spread, dot_nn)
+    rows = [lines[row // 3 : row // 3 + 1, row % 3 * 128 : row % 3 * 128 + 128] for row in range(8)]
+    return jnp.concatenate(rows, axis=0)
+
+
+class Compute:
+    def __init__(self, w, vrows, gvec, red):
+        self.w = w
+        self.vrows = vrows
+        self.gvec = gvec
+        self.red = red
+
+    def vec(self, index):
+        return self.vrows[pl.ds(index, 1), :]
+
+    def norm(self, src, src_row, dst, dst_row, rows, gain, shift, unit, unit_row, rate, rate_row):
+        scale_vec, shift_vec = self.vec(gain), self.vec(shift)
+
+        @pl.loop(0, rows // NORM_ROWS)
+        def _(index):
+            x = src[chunk(src_row + index * NORM_ROWS, NORM_ROWS), :].astype(F32)
+            centre = x - jnp.mean(x, axis=-1, keepdims=True)
+            spread = jnp.mean(centre * centre, axis=-1, keepdims=True)
+            scale = lax.rsqrt(spread + 1e-06)
+            even = centre * scale
+            result = even * scale_vec + shift_vec
+            dst[chunk(dst_row + index * NORM_ROWS, NORM_ROWS), :] = result.astype(BF16)
+            if unit is not None:
+                unit[chunk(unit_row + index * NORM_ROWS, NORM_ROWS), :] = even.astype(unit.dtype)
+            rate[chunk(rate_row + index * NORM_ROWS, NORM_ROWS), :] = jnp.broadcast_to(
+                scale, (NORM_ROWS, 128)
+            )
+
+    def unit_rows(self, src, rows):
+        @pl.loop(0, rows // NORM_ROWS)
+        def _(index):
+            at = chunk(index * NORM_ROWS, NORM_ROWS)
+            x = src[at, :].astype(F32)
+            centre = x - jnp.mean(x, axis=-1, keepdims=True)
+            spread = jnp.mean(centre * centre, axis=-1, keepdims=True)
+            src[at, :] = (centre * lax.rsqrt(spread + 1e-06)).astype(src.dtype)
+
+    def norm_back(
+        self, unit, unit_row, rate, rate_row, grad, rest, out, low, rows, gain, shift
+    ):
+        scale_vec = self.vec(gain)
+        self.red[...] = jnp.zeros_like(self.red)
+
+        @pl.loop(0, rows // NORM_ROWS)
+        def _(index):
+            at = chunk(index * NORM_ROWS, NORM_ROWS)
+            even = unit[chunk(unit_row + index * NORM_ROWS, NORM_ROWS), :].astype(F32)
+            scale = rate[chunk(rate_row + index * NORM_ROWS, NORM_ROWS), 0:1]
+            d = grad[at, :]
+            along = d * even
+            self.red[0] += jnp.sum(along.reshape(NORM_ROWS // 8, 8, D), axis=0)
+            self.red[1] += jnp.sum(d.reshape(NORM_ROWS // 8, 8, D), axis=0)
+            d = d * scale_vec
+            mean = jnp.mean(d, axis=-1, keepdims=True)
+            along = jnp.mean(along * scale_vec, axis=-1, keepdims=True)
+            total = rest[at, :].astype(F32) + scale * (d - mean - even * along)
+            if out is not None:
+                out[at, :] = total
+            if low is not None:
+                low[at, :] = total.astype(BF16)
+
+        self.gvec[pl.ds(gain, 1), :] = jnp.sum(self.red[0], axis=0, keepdims=True)
+        self.gvec[pl.ds(shift, 1), :] = jnp.sum(self.red[1], axis=0, keepdims=True)
+
+    def row_sum(self, values):
+        ones = jnp.ones((TILE, values.shape[0]), BF16)
+        return dot_nn(ones, values)[0:1]
+
+    def linear(self, src, row, rows, index, bias, emit):
+        @pl.loop(0, D // BLOCK, unroll=UNROLL)
+        def _(part):
+            cols = chunk(part * BLOCK)
+            made = dot_nn(src[pl.ds(row, rows), :], self.w[chunk(index * D, D), cols])
+            if bias is not None:
+                made = made + self.vrows[pl.ds(bias, 1), cols]
+            emit(cols, made)
+
+    def linear_back(self, pairs, emit):
+        @pl.loop(0, D // BLOCK, unroll=UNROLL)
+        def _(part):
+            total = None
+            for grad, index in pairs:
+                made = dot_nt(grad(), self.w[chunk(index * D + part * BLOCK), :])
+                total = made if total is None else total + made
+            emit(chunk(part * BLOCK), total)
+
+    def weight_grad(self, left, right, index, parts=D // BLOCK):
+        @pl.loop(0, parts, unroll=UNROLL)
+        def _(part):
+            total = None
+            for one, other in zip(left(part), right):
+                made = dot_tn(one, other())
+                total = made if total is None else total + made
+            self.w[chunk(index * D + part * BLOCK), :] = total.astype(BF16)
+
+    def hidden(self, src, row, rows, first, bias, act, slope, pieces=(0, FF // D)):
+        each = D // BLOCK
+
+        @pl.loop(pieces[0] * each, pieces[1] * each, unroll=UNROLL)
+        def _(part):
+            piece = lax.div(part, each)
+            u = dot_nt(src[pl.ds(row, rows), :], self.w[chunk(first * D + part * BLOCK), :])
+            u = u + self.vrows[pl.ds(bias + piece, 1), chunk(lax.rem(part, each) * BLOCK)]
+            square = u * u
+            t = jnp.tanh(u * (0.7978845608028654 + 0.035677408136300125 * square))
+            half = 0.5 + 0.5 * t
+            at = (pl.ds(0, rows), chunk(part * BLOCK))
+            made = u * half
+            act[at] = made.astype(BF16)
+            rise = 1.5957691216057308 + 0.21406444881780074 * square
+            slope[at] = (half + made * (1.0 - half) * rise).astype(BF16)
+
+    def project(self, act, rows, first, emit):
+        @pl.loop(0, D // BLOCK)
+        def _(part):
+            cols = chunk(part * BLOCK)
+            emit(cols, dot_nn(act[pl.ds(0, rows), :], self.w[chunk(first * D, FF), cols]))
+
+    def hidden_back(self, low, rows, first, slope):
+        @pl.loop(0, FF // BLOCK, unroll=UNROLL)
+        def _(part):
+            made = dot_nt(low[pl.ds(0, rows), :], self.w[chunk(first * D + part * BLOCK), :])
+            at = (pl.ds(0, rows), chunk(part * BLOCK))
+            slope[at] = (made * slope[at].astype(F32)).astype(BF16)
+
+    def wide_grad(self, left, rows, right, first):
+        self.weight_grad(
+            lambda part: [left[pl.ds(0, rows), chunk(part * BLOCK)]], [right], first, FF // BLOCK
+        )
+
+    def wide_sums(self, slope, rows, bias):
+        for piece in range(FF // D):
+            self.gvec[pl.ds(bias + piece, 1), :] = self.row_sum(
+                slope[pl.ds(0, rows), pl.ds(piece * D, D)]
+            )
+
+    @staticmethod
+    def halves(tile, scale=1.0):
+        low = jnp.where(iota(tile.shape, 1) < HEAD, scale, 0.0).astype(BF16)
+        high = jnp.where(iota(tile.shape, 1) < HEAD, 0.0, scale).astype(BF16)
+        return tile * low, tile * high
+
+    def attend(self, allowed, q_at, k_at, v_at, p_at, o_at):
+        @pl.loop(0, PAIRS, unroll=ATTEND_UNROLL)
+        def _(pair):
+            keys = k_at(pair)[...]
+            values = v_at(pair)[...].T
+            mixed = []
+            for half, queries in enumerate(self.halves(q_at(pair)[...], 0.125)):
+                scores = jnp.where(allowed, dot_nt(keys, queries), -1000000000.0)
+                expd = jnp.exp(scores - jnp.max(scores, axis=0, keepdims=True))
+                rate = 1.0 / jnp.sum(expd, axis=0, keepdims=True)
+                probs = (expd * rate).astype(BF16)
+                p_at(pair, half)[...] = probs
+                mixed.append(dot_nn(values, probs)[half * HEAD : (half + 1) * HEAD])
+            o_at(pair)[...] = jnp.concatenate(mixed, axis=0).T.astype(BF16)
+
+    def attend_back(self, q_at, k_at, v_at, p_at, do_at):
+        @pl.loop(0, PAIRS, unroll=ATTEND_UNROLL)
+        def _(pair):
+            keys = k_at(pair)[...].T
+            values = v_at(pair)[...]
+            grad_q, grad_k, grad_v = [], 0.0, 0.0
+            both = zip(self.halves(q_at(pair)[...], 0.125), self.halves(do_at(pair)[...]))
+            for half, (queries, grads) in enumerate(both):
+                low = p_at(pair, half)[...]
+                probs = low.astype(F32)
+                grad_probs = dot_nt(values, grads)
+                inner = jnp.sum(probs * grad_probs, axis=0, keepdims=True)
+                grad_scores = (probs * (grad_probs - inner)).astype(BF16)
+                grad_q.append(dot_nn(keys, grad_scores)[half * HEAD : (half + 1) * HEAD])
+                grad_k = grad_k + dot_nn(grad_scores, queries)
+                grad_v = grad_v + dot_nn(low, grads)
+            q_at(pair)[...] = (jnp.concatenate(grad_q, axis=0) * 0.125).T.astype(BF16)
+            k_at(pair)[...] = grad_k.astype(BF16)
+            v_at(pair)[...] = grad_v.astype(BF16)
+
+
+def store_to(ref, row, rows, col=0):
+    def emit(cols, values):
+        ref[pl.ds(row, rows), chunk(col + cols.start)] = values.astype(ref.dtype)
+
+    return emit
+
+
+def fused_kernel(
+    depth,
+    sizes,
+    pers,
+    slots,
+    words,
+    images_in,
+    enc_cot,
+    tissue,
+    text_len,
+    text_in,
+    enc_in,
+    dec_in,
+    enc_tile,
+    dec_tile,
+    dec_cot,
+    enc_out,
+    dec_out,
+    image_out,
+    text_out,
+    enc_g,
+    dec_g,
+    enc_v,
+    dec_v,
+    w,
+    land,
+    xin,
+    n1,
+    q,
+    k,
+    v,
+    o,
+    h,
+    n2,
+    act,
+    gp,
+    e,
+    cot,
+    acc,
+    dh,
+    low,
+    dmix,
+    keep_col,
+    rates,
+    tiles,
+    vrows,
+    gvec,
+    vland,
+    vout,
+    red,
+    load_sems,
+    ag_send,
+    ag_recv,
+    vec_send,
+    vec_recv,
+    rs_send,
+    rs_recv,
+    sum_send,
+    sum_recv,
+    x_send,
+    x_recv,
+    out_local,
+    out_send,
+    out_recv,
+    gate_sem,
+):
+    shards = depth * 4
+    place = Place(depth)
+    me, z = place.me, place.z
+    section = place.section
+    image_rows, text_rows = xin.shape[0], text_in.shape[0]
+    images, used = tissue.shape
+    comp = Compute(w, vrows, gvec, red)
+    cuts = [split_rows(rows, LATE) for rows in sizes]
+
+    def load(index, src, dst, waiting=False):
+        copy = pltpu.make_async_copy(src, dst, load_sems.at[index])
+        if waiting:
+            copy.wait()
+        else:
+            copy.start()
+
+    def own_rows(which):
+        return w.at[pl.ds(pl.multiple_of(me * sizes[which], TILE), sizes[which])]
+
+    def load_own(which, waiting):
+        load(0, (enc_in, dec_in)[which], own_rows(which), waiting)
+        load(1, (enc_tile, dec_tile)[which], tiles.at[me], waiting)
+
+    def load_text(waiting):
+        load(2, text_in, xin.at[pl.ds(0, text_rows)], waiting)
+        load(3, dec_cot, low.at[pl.ds(0, text_rows)], waiting)
+
+    for which in (0, 1):
+
+        @pl.when(section == which)
+        def _():
+            load_own(which, False)
+            if which == 1:
+                load_text(False)
+
+    greet(place, shards, True)
+
+    def give_vecs(waiting):
+        src = tiles.at[me]
+        for step in range(1, shards):
+            Copies(place, waiting).start(
+                None, src, src, vec_send.at[step], vec_recv.at[me], lax.rem(me + step, shards)
+            )
+
+    def got_vecs():
+        for step in range(1, shards):
+            frm = lax.rem(me + step, shards)
+            Copies(place).arrived(tiles.at[frm], vec_send.at[step], vec_recv.at[frm])
+
+    def across(waiting, index, src, dst):
+        Copies(place, waiting).start(
+            None, src, dst, x_send.at[index], x_recv.at[index], me, 1 - section
+        )
+
+    def crossed(index, dst):
+        Copies(place).arrived(dst, x_send.at[index], x_recv.at[index])
+
+    def give(waiting, index, src, dst):
+        local = pltpu.make_async_copy(src, dst, out_local.at[index])
+        if waiting:
+            local.wait()
+        else:
+            local.start()
+        Copies(place, waiting).start(
+            None, src, dst, out_send.at[index], out_recv.at[index], me, 1 - section
+        )
+
+    def got(index, dst):
+        Copies(place).arrived(dst, out_send.at[index], out_recv.at[index])
+
+    def share_sums(waiting, slot, to):
+        Copies(place, waiting).start(
+            None, gvec, vland.at[slot], sum_send.at[slot], sum_recv.at[slot], to
+        )
+
+    def got_sums(slot):
+        Copies(place).arrived(vland.at[slot], sum_send.at[slot], sum_recv.at[slot])
+
+    def open_gate():
+        pl.semaphore_signal(
+            gate_sem, inc=1, device_id=(1 - section, me), device_id_type=MESH
+        )
+
+    def pass_gate():
+        pl.semaphore_wait(gate_sem, 1)
+
+    flips = (place.shard(z, place.y, 1 - place.x), place.shard(z, 1 - place.y, place.x))
+
+    def sum_stages(which):
+        def along_x():
+            share_sums(False, 0, flips[0])
+
+        def along_y():
+            got_sums(0)
+            share_sums(True, 0, flips[0])
+            gvec[...] = gvec[...] + vland[0]
+            share_sums(False, 1, flips[1])
+
+        def along_z():
+            got_sums(1)
+            share_sums(True, 1, flips[1])
+            gvec[...] = gvec[...] + vland[1]
+            for step in range(1, depth):
+                share_sums(False, 1 + step, lax.rem(me + 4 * step, shards))
+
+        def ended():
+            summed = gvec[...]
+            for step in range(1, depth):
+                got_sums(1 + step)
+                share_sums(True, 1 + step, lax.rem(me + 4 * step, shards))
+                summed = summed + vland[1 + step]
+            vout[...] = vec_shard(summed, me, pers[which])
+            give(False, 6, vout, (enc_v, dec_v)[which])
+
+        return {30: along_x, 31: along_y, 32: along_z, 33: ended}
+
+    def gather(which, waiting=False):
+        return Gather(
+            Copies(place, waiting),
+            place,
+            depth,
+            sizes[which],
+            cuts[which],
+            w,
+            ag_send,
+            ag_recv,
+            open_gate if which == 0 else pass_gate,
+        )
+
+    def give_class(waiting, which, cls):
+        start, size = cuts[which][cls]
+        if size:
+            src = w.at[pl.ds(pl.multiple_of(me * sizes[which] + start, TILE), size)]
+            give(waiting, 2 + cls, src, (enc_g, dec_g)[which].at[pl.ds(start, size)])
+
+    def got_class(which, cls):
+        start, size = cuts[which][cls]
+        if size:
+            got(2 + cls, (enc_g, dec_g)[which].at[pl.ds(start, size)])
+
+    def scatter(which, waiting=False):
+        return Scatter(
+            Copies(place, waiting),
+            place,
+            depth,
+            sizes[which],
+            cuts[which],
+            w,
+            land,
+            rs_send,
+            rs_recv,
+            functools.partial(give_class, False, which),
+        )
+
+    def start_stage(which):
+        got_vecs()
+        vrows[...] = vec_gathered(tiles, pers[which])
+        gvec[...] = jnp.zeros_like(gvec)
+
+    def padded(src):
+        row = iota((image_rows, src.shape[0]), 0)
+        slot = row & (slots - 1)
+        frm = lax.shift_right_logical(row, 8) * used + slot
+        pick = (iota((image_rows, src.shape[0]), 1) == frm) & (slot < used)
+        return dot_nn(pick.astype(F32).astype(BF16), src[...]).astype(BF16)
+
+    def fill_keep():
+        keep_col[...] = jnp.zeros_like(keep_col)
+        for image in range(images):
+            line = tissue[pl.ds(image, 1), :].astype(F32).astype(BF16)
+            lines = jnp.broadcast_to(line, (TILE, used))
+            keep_col[pl.ds(image * slots, used), :] = dot_tn(
+                lines, jnp.full((TILE, 128), 1.0 / TILE, BF16)
+            )
+
+    def spread(column, wide):
+        return jnp.concatenate([column] * (wide // 128), axis=1) > 0.5
+
+    def section_program(which, make):
+        stages = sum_stages(which)
+        gathering = Plan(GATHER_PLANS[which], gather(which), gather(which, True), stages)
+        scattering = Plan(SCATTER_PLANS[which], scatter(which), scatter(which, True), stages)
+
+        def gathered():
+            gathering.flush()
+            give_vecs(True)
+
+        made, last = make(gathered)
+        stages.update(made)
+        load_own(which, True)
+        gathering.run()
+        scattering.run()
+        scattering.flush()
+        for cls in range(4):
+            give_class(True, which, cls)
+        give(True, 6, vout, (enc_v, dec_v)[which])
+        last()
+        for cls in range(4):
+            got_class(1 - which, cls)
+        got(6, (enc_v, dec_v)[1 - which])
+
+    def encoder(gathered):
+        rows = image_rows
+        every = pl.ds(0, rows)
+        stages = {}
+
+        def stage(number):
+            def keep(step):
+                stages[number] = step
+                return step
+
+            return keep
+
+        spare = shards * sizes[0]
+
+        def at(ref, image):
+            return lambda pair: ref.at[pl.ds(image * slots, slots), chunk(pair * 128, 128)]
+
+        def p_at(image):
+            def of(pair, half):
+                index = (image * PAIRS + pair) * 2 + half
+                row = spare + lax.div(index, 3) * slots
+                return w.at[chunk(row, slots), chunk(lax.rem(index, 3) * slots, slots)]
+
+            return of
+
+        stages[8] = lambda: give_vecs(False)
+
+        @stage(0)
+        def _():
+            fill_keep()
+            xin[...] = padded(images_in)
+            start_stage(0)
+            comp.norm(xin, 0, n1, 0, rows, 0, 1, None, 0, rates.at[0], 0)
+
+        @stage(1)
+        def _():
+            comp.linear(n1, 0, rows, 0, 2, store_to(q, 0, rows))
+            comp.linear(n1, 0, rows, 1, None, store_to(k, 0, rows))
+            comp.linear(n1, 0, rows, 2, 3, store_to(v, 0, rows))
+
+        @stage(2)
+        def _():
+            for image in range(images):
+                allowed = spread(keep_col[pl.ds(image * slots, slots), :], slots)
+                comp.attend(
+                    allowed, at(q, image), at(k, image), at(v, image), p_at(image), at(o, image)
+                )
+
+        @stage(3)
+        def _():
+            def add_input(cols, values):
+                h[every, cols] = xin[every, cols].astype(F32) + values
+
+            comp.linear(o, 0, rows, 3, 4, add_input)
+            comp.norm(h, 0, n2, 0, rows, 5, 6, dh, 0, rates.at[1], 0)
+
+        @stage(4)
+        def _():
+            comp.hidden(n2, 0, rows, 4, 8, act, gp, (0, 2))
+
+        @stage(5)
+        def _():
+            comp.hidden(n2, 0, rows, 4, 8, act, gp, (2, 4))
+
+        @stage(6)
+        def _():
+            def add_middle(cols, values):
+                keep = jnp.concatenate([keep_col[...]] * (BLOCK // 128), axis=1)
+                made = h[every, cols] + values + vrows[pl.ds(7, 1), cols]
+                e[every, cols] = (made * keep).astype(BF16)
+
+            comp.project(act, rows, 8, add_middle)
+            across(False, 0, e, e)
+            load(5, e, enc_out)
+
+        @stage(7)
+        def _():
+            gathered()
+
+            comp.unit_rows(xin, rows)
+
+        @stage(10)
+        def _():
+            crossed(1, cot)
+
+            @pl.loop(0, rows // LINES)
+            def _(index):
+                some = chunk(index * LINES, LINES)
+                low[some, :] = (cot[some, :].astype(F32) * keep_col[some, 0:1]).astype(BF16)
+
+            gvec[pl.ds(7, 1), :] = comp.row_sum(low[...])
+
+        @stage(11)
+        def _():
+            comp.hidden_back(low, rows, 8, gp)
+
+        @stage(12)
+        def _():
+            comp.wide_grad(act, rows, lambda: low[...], 8)
+
+        @stage(13)
+        def _():
+            comp.project(gp, rows, 4, store_to(acc, 0, rows))
+
+        @stage(14)
+        def _():
+            comp.wide_sums(gp, rows, 8)
+            comp.wide_grad(gp, rows, lambda: n2[...], 4)
+
+        @stage(15)
+        def _():
+            comp.norm_back(dh, 0, rates.at[1], 0, acc, low, dh, low, rows, 5, 6)
+
+        @stage(16)
+        def _():
+            comp.linear_back([(lambda: low[...], 3)], store_to(dmix, 0, rows))
+
+        @stage(17)
+        def _():
+            gvec[pl.ds(4, 1), :] = comp.row_sum(low[...])
+            comp.weight_grad(lambda part: [o[:, chunk(part * BLOCK)]], [lambda: low[...]], 3)
+
+        def heads_back(image):
+            comp.attend_back(
+                at(q, image), at(k, image), at(v, image), p_at(image), at(dmix, image)
+            )
+
+        stages[18] = lambda: heads_back(0)
+        stages[19] = lambda: [heads_back(image) for image in range(1, images)]
+
+        @stage(20)
+        def _():
+            comp.linear_back(
+                [(lambda: q[...], 0), (lambda: k[...], 1), (lambda: v[...], 2)],
+                store_to(acc, 0, rows),
+            )
+
+        @stage(21)
+        def _():
+            gvec[pl.ds(2, 1), :] = comp.row_sum(q[...])
+            gvec[pl.ds(3, 1), :] = comp.row_sum(v[...])
+            for index, ref in enumerate((q, k, v)):
+                comp.weight_grad(
+                    lambda part: [n1[:, chunk(part * BLOCK)]], [lambda: ref[...]], index
+                )
+
+        @stage(22)
+        def _():
+            comp.norm_back(xin, 0, rates.at[0], 0, acc, dh, None, low, rows, 0, 1)
+            give(False, 1, low, image_out)
+
+        def last():
+            across(True, 0, e, e)
+            load(5, e, enc_out, True)
+            give(True, 1, low, image_out)
+            got(0, dec_out)
+            got(1, text_out)
+
+        return stages, last
+
+    def decoder(gathered):
+        half = text_rows
+        lower, upper = pl.ds(0, half), pl.ds(half, half)
+        stages = {}
+
+        def stage(number):
+            def keep(step):
+                stages[number] = step
+                return step
+
+            return keep
+
+        def at(ref, image, base=0):
+            return lambda pair: ref.at[
+                pl.ds(base + image * words, words), chunk(pair * 128, 128)
+            ]
+
+        def p_self(image):
+            ref = (k, v)[image]
+
+            def of(pair, side):
+                row = half + lax.div(pair, 3) * words
+                return ref.at[
+                    chunk(row, words), chunk((lax.rem(pair, 3) * 2 + side) * words, words)
+                ]
+
+            return of
+
+        def p_cross(image):
+            return lambda pair, side: act.at[
+                upper, chunk(((image * PAIRS + pair) * 2 + side) * words, words)
+            ]
+
+        def cross_kv(image, which):
+            col = (which * images + image) * D
+            return lambda pair: gp.at[pl.ds(half, slots), chunk(col + pair * 128, 128)]
+
+        def pair_ref(image, which):
+            return lambda: gp[pl.ds(half, slots), pl.ds((which * images + image) * D, D)]
+
+        def low_rows():
+            return low[lower, :]
+
+        dz = dmix.at[upper]
+        decoded = xin.at[upper]
+        text_grad = low.at[upper]
+
+        stages[29] = lambda: give_vecs(False)
+
+        @stage(0)
+        def _():
+            load_text(True)
+            fill_keep()
+            cot[...] = padded(enc_cot)
+            start_stage(1)
+            comp.norm(xin, 0, n1, 0, half, 0, 1, n1, half, rates.at[0], 0)
+
+        @stage(1)
+        def _():
+            comp.linear(n1, 0, half, 0, 2, store_to(q, 0, half))
+            comp.linear(n1, 0, half, 1, None, store_to(k, 0, half))
+            comp.linear(n1, 0, half, 2, 3, store_to(v, 0, half))
+
+        @stage(2)
+        def _():
+            key, query = iota((words, words), 0), iota((words, words), 1)
+            for image in range(images):
+                allowed = (key <= query) & (key < text_len[image])
+                comp.attend(
+                    allowed, at(q, image), at(k, image), at(v, image), p_self(image), at(o, image)
+                )
+
+        @stage(3)
+        def _():
+            def add_input(cols, values):
+                h[lower, cols] = xin[lower, cols].astype(F32) + values
+
+            comp.linear(o, 0, half, 3, 4, add_input)
+            comp.norm(h, 0, n2, 0, half, 5, 6, acc, half, rates.at[1], 0)
+
+        @stage(4)
+        def _():
+            comp.linear(n2, 0, half, 4, 7, store_to(q, half, half))
+
+        @stage(5)
+        def _():
+            crossed(0, e)
+            load(5, e, enc_out)
+            for image in range(images):
+                row = image * slots
+                comp.linear(e, row, slots, 5, None, store_to(gp, half, slots, image * D))
+                comp.linear(e, row, slots, 6, 8, store_to(gp, half, slots, (images + image) * D))
+
+        @stage(6)
+        def _():
+            for image in range(images):
+                allowed = spread(keep_col[pl.ds(image * slots, slots), :], words)
+                comp.attend(
+                    allowed,
+                    at(q, image, half),
+                    cross_kv(image, 0),
+                    cross_kv(image, 1),
+                    p_cross(image),
+                    at(o, image, half),
+                )
+
+        @stage(7)
+        def _():
+            def add_self(cols, values):
+                h[upper, cols] = h[lower, cols] + values
+
+            comp.linear(o, half, half, 7, 9, add_self)
+            comp.norm(h, half, n2, half, half, 10, 11, dh, half, rates.at[2], 0)
+
+        @stage(8)
+        def _():
+            comp.hidden(n2, half, half, 8, 13, act, gp)
+
+        @stage(9)
+        def _():
+            def add_middle(cols, values):
+                made = h[upper, cols] + values + vrows[pl.ds(12, 1), cols]
+                xin[upper, cols] = made.astype(BF16)
+
+            comp.project(act.at[lower], half, 12, add_middle)
+            give(False, 0, decoded, dec_out)
+
+        @stage(10)
+        def _():
+            comp.hidden_back(low, half, 12, gp)
+            dz[...] = low_rows()
+
+        @stage(11)
+        def _():
+            gathered()
+            gvec[pl.ds(12, 1), :] = comp.row_sum(dz[...])
+            comp.wide_grad(act, half, lambda: dz[...], 12)
+
+        @stage(12)
+        def _():
+            comp.project(gp.at[lower], half, 8, store_to(acc, 0, half))
+
+        @stage(13)
+        def _():
+            comp.wide_sums(gp, half, 13)
+            comp.wide_grad(gp, half, lambda: n2[upper, :], 8)
+
+        @stage(14)
+        def _():
+            comp.norm_back(dh, half, rates.at[2], 0, acc, low, dh, low, half, 10, 11)
+            comp.linear_back([(low_rows, 7)], store_to(dmix, 0, half))
+
+        @stage(15)
+        def _():
+            for image in range(images):
+                comp.attend_back(
+                    at(q, image, half),
+                    cross_kv(image, 0),
+                    cross_kv(image, 1),
+                    p_cross(image),
+                    at(dmix, image),
+                )
+
+        @stage(16)
+        def _():
+            for image in range(images):
+                rows = pl.ds(image * slots, slots)
+
+                def add_cot(cols, values):
+                    cot[rows, cols] = (cot[rows, cols].astype(F32) + values).astype(BF16)
+
+                comp.linear_back([(pair_ref(image, 0), 5), (pair_ref(image, 1), 6)], add_cot)
+            across(False, 1, cot, cot)
+
+        @stage(17)
+        def _():
+            gvec[pl.ds(9, 1), :] = comp.row_sum(low_rows())
+            comp.weight_grad(lambda part: [o[upper, chunk(part * BLOCK)]], [low_rows], 7)
+
+        @stage(18)
+        def _():
+            comp.linear_back([(lambda: q[upper, :], 4)], store_to(acc, 0, half))
+
+        @stage(19)
+        def _():
+            gvec[pl.ds(7, 1), :] = comp.row_sum(q[upper, :])
+            total = comp.row_sum(pair_ref(0, 1)())
+            for image in range(1, images):
+                total = total + comp.row_sum(pair_ref(image, 1)())
+            gvec[pl.ds(8, 1), :] = total
+            comp.weight_grad(
+                lambda part: [n2[lower, chunk(part * BLOCK)]], [lambda: q[upper, :]], 4
+            )
+            for which in (0, 1):
+                comp.weight_grad(
+                    lambda part: [
+                        e[pl.ds(image * slots, slots), chunk(part * BLOCK)]
+                        for image in range(images)
+                    ],
+                    [pair_ref(image, which) for image in range(images)],
+                    5 + which,
+                )
+
+        @stage(20)
+        def _():
+            comp.norm_back(acc, half, rates.at[1], 0, acc, dh, dh, low, half, 5, 6)
+
+        @stage(21)
+        def _():
+            comp.linear_back([(low_rows, 3)], store_to(dmix, 0, half))
+
+        @stage(22)
+        def _():
+            gvec[pl.ds(4, 1), :] = comp.row_sum(low_rows())
+            comp.weight_grad(lambda part: [o[lower, chunk(part * BLOCK)]], [low_rows], 3)
+
+        @stage(23)
+        def _():
+            for image in range(images):
+                comp.attend_back(
+                    at(q, image), at(k, image), at(v, image), p_self(image), at(dmix, image)
+                )
+
+        @stage(24)
+        def _():
+            comp.linear_back(
+                [(lambda: q[lower, :], 0), (lambda: k[lower, :], 1), (lambda: v[lower, :], 2)],
+                store_to(acc, 0, half),
+            )
+
+        @stage(25)
+        def _():
+            gvec[pl.ds(2, 1), :] = comp.row_sum(q[lower, :])
+            gvec[pl.ds(3, 1), :] = comp.row_sum(v[lower, :])
+            for index, ref in enumerate((q, k, v)):
+                comp.weight_grad(
+                    lambda part: [n1[lower, chunk(part * BLOCK)]], [lambda: ref[lower, :]], index
+                )
+
+        @stage(26)
+        def _():
+            comp.norm_back(n1, half, rates.at[0], 0, acc, dh, None, text_grad, half, 0, 1)
+            give(False, 1, text_grad, text_out)
+
+        def last():
+            across(True, 1, cot, cot)
+            load(5, e, enc_out, True)
+            give(True, 0, decoded, dec_out)
+            give(True, 1, text_grad, text_out)
+            got(1, image_out)
+
+        return stages, last
+
+    pl.when(section == 0)(lambda: section_program(0, encoder))
+    pl.when(section == 1)(lambda: section_program(1, decoder))
+
+
+def finish_kernel(
+    used, encoded, decoded, images, text, enc, dec, enc_v, dec_v, *outs
+):
+    enc_out, dec_out, image_out, text_out, enc_out_g, dec_out_g, enc_out_v, dec_out_v = outs
+    slots = BLOCK
+
+    def cut(ref):
+        rows = ref[...].astype(F32)
+        parts = [
+            rows[image * slots : image * slots + used] for image in range(rows.shape[0] // slots)
+        ]
+        return jnp.concatenate(parts, axis=0)
+
+    @pl.when(pl.program_id(0) == 0)
+    def _():
+        enc_out[...] = cut(encoded).astype(BF16)
+        image_out[...] = cut(images)
+        enc_out_v[...] = in_line(enc_v[...])
+        dec_out_v[...] = in_line(dec_v[...])
+
+    dec_out[...] = decoded[...]
+    text_out[...] = text[...].astype(F32)
+    enc_out_g[...] = enc[...].astype(F32)
+    dec_out_g[...] = dec[...].astype(F32)
+
+
+def vec_tile_of(vecs):
+    units = vecs.reshape(-1, VEC_UNIT)
+    return jnp.pad(units, ((0, VEC_ROWS - units.shape[0]), (0, 128 - VEC_UNIT)))
+
+
+def body_fast(
+    images, text, enc_mats, enc_vecs, dec_mats, dec_vecs, tissue, text_len, enc_cot, dec_cot
+):
+    shards = lax.axis_size("dp")
+    depth = grid_of(shards)[0]
+    img_count, slots = tissue.shape
+    words = text.shape[0] // img_count
+    sizes = (enc_mats.shape[0], dec_mats.shape[0])
+    pers = (enc_vecs.shape[0] // VEC_UNIT, dec_vecs.shape[0] // VEC_UNIT)
+    wide = BLOCK
+    image_rows, text_rows = img_count * wide, img_count * words
+    any_space = pl.BlockSpec(memory_space=pl.ANY)
+    vmem_space = pl.BlockSpec(memory_space=pltpu.VMEM)
+    smem_space = pl.BlockSpec(memory_space=pltpu.SMEM)
+    most = sizes[1]
+
+    def low_buffer(rows=image_rows, columns=D):
+        return pltpu.VMEM((rows, columns), BF16)
+
+    def wide_buffer(rows=image_rows):
+        return pltpu.VMEM((rows, D), F32)
+
+    dma = pltpu.SemaphoreType.DMA
+    made = pl.pallas_call(
+        functools.partial(fused_kernel, depth, sizes, pers, wide, words),
+        out_shape=(
+            jax.ShapeDtypeStruct((image_rows, D), BF16),
+            jax.ShapeDtypeStruct((text_rows, D), BF16),
+            jax.ShapeDtypeStruct((image_rows, D), BF16),
+            jax.ShapeDtypeStruct((text_rows, D), BF16),
+            jax.ShapeDtypeStruct((sizes[0], D), BF16),
+            jax.ShapeDtypeStruct((sizes[1], D), BF16),
+            jax.ShapeDtypeStruct((VEC_ROWS, 128), F32),
+            jax.ShapeDtypeStruct((VEC_ROWS, 128), F32),
+        ),
+        in_specs=[vmem_space] * 3 + [smem_space] + [any_space] * 6,
+        out_specs=[any_space] * 8,
+        scratch_shapes=[
+            low_buffer(shards * most),
+            low_buffer(max(Scatter.land_rows(depth, split_rows(rows, LATE)) for rows in sizes)),
+            low_buffer(),
+            low_buffer(),
+            low_buffer(),
+            low_buffer(),
+            low_buffer(),
+            low_buffer(),
+            wide_buffer(),
+            low_buffer(),
+            low_buffer(image_rows, FF),
+            low_buffer(image_rows, FF),
+            low_buffer(),
+            low_buffer(),
+            wide_buffer(),
+            wide_buffer(),
+            low_buffer(),
+            low_buffer(),
+            pltpu.VMEM((image_rows, 128), F32),
+            pltpu.VMEM((3, image_rows, 128), F32),
+            pltpu.VMEM((shards, VEC_ROWS, 128), BF16),
+            wide_buffer(VEC_ROWS),
+            wide_buffer(VEC_ROWS),
+            pltpu.VMEM((1 + depth, VEC_ROWS, D), F32),
+            pltpu.VMEM((VEC_ROWS, 128), F32),
+            pltpu.VMEM((2, 8, D), F32),
+            dma((6,)),
+            dma((4, shards, 4)),
+            dma((4, shards)),
+            dma((shards,)),
+            dma((shards,)),
+            dma((4, 4 * depth + 7)),
+            dma((4, 4 * depth + 7)),
+            dma((1 + depth,)),
+            dma((1 + depth,)),
+            dma((2,)),
+            dma((2,)),
+            dma((7,)),
+            dma((7,)),
+            dma((7,)),
+            pltpu.SemaphoreType.REGULAR,
+        ],
+        compiler_params=pltpu.CompilerParams(
+            collective_id=0, has_side_effects=True, vmem_limit_bytes=VMEM_LIMIT
+        ),
+        name="blocks_and_grads",
+    )(
+        images,
+        enc_cot,
+        tissue,
+        text_len,
+        text,
+        enc_mats,
+        dec_mats,
+        vec_tile_of(enc_vecs),
+        vec_tile_of(dec_vecs),
+        dec_cot,
+    )
+
+    def tiled(rows):
+        return pl.BlockSpec((rows // FINISH_STEPS, D), lambda step: (step, 0))
+
+    def whole(shape):
+        return pl.BlockSpec(shape, lambda step: (0, 0))
+
+    image_spec, tile_spec = whole((image_rows, D)), whole((VEC_ROWS, 128))
+    out_spec = whole((img_count * slots, D))
+    outs = pl.pallas_call(
+        functools.partial(finish_kernel, slots),
+        grid=(FINISH_STEPS,),
+        in_specs=[
+            image_spec,
+            tiled(text_rows),
+            image_spec,
+            tiled(text_rows),
+            tiled(sizes[0]),
+            tiled(sizes[1]),
+            tile_spec,
+            tile_spec,
+        ],
+        out_specs=[
+            out_spec,
+            tiled(text_rows),
+            out_spec,
+            tiled(text_rows),
+            tiled(sizes[0]),
+            tiled(sizes[1]),
+            whole((8, 128)),
+            whole((8, 128)),
+        ],
+        out_shape=(
+            jax.ShapeDtypeStruct((img_count * slots, D), BF16),
+            jax.ShapeDtypeStruct((text_rows, D), BF16),
+            jax.ShapeDtypeStruct((img_count * slots, D), F32),
+            jax.ShapeDtypeStruct((text_rows, D), F32),
+            jax.ShapeDtypeStruct((sizes[0], D), F32),
+            jax.ShapeDtypeStruct((sizes[1], D), F32),
+            jax.ShapeDtypeStruct((8, 128), F32),
+            jax.ShapeDtypeStruct((8, 128), F32),
+        ),
+        name="finish_outputs",
+    )(*made)
+
+    def vec_of(tile, per):
+        return tile.reshape(-1)[: per * VEC_UNIT]
+
+    return (
+        outs[0],
+        outs[1],
+        outs[2],
+        outs[3],
+        outs[4],
+        vec_of(outs[6], pers[0]),
+        outs[5],
+        vec_of(outs[7], pers[1]),
+    )
+
+
+FINISH_STEPS = 4
+VMEM_LIMIT = 63 * 2**20
+LATE = 0.21
+GATHER_PLANS = (
+    (
+        120, 110, 400, 100, 130, 500, 121, 131, 8, 101, 111, 200, 231, 620, 630, 230, 102, 1500,
+        221, 112, 201, 600, 631, 621, 601, 0, 103, 122, 211, 202, 132, 203, 610, 602, 603, 300,
+        212, 220, 210, 611, 133, 1, 222, 2, 233, 632, 622, 612, 232, 310, 3, 4, 320, 5, 633, 330,
+    ),
+    (
+        400, 500, 110, 130, 630, 100, 120, 101, 121, 102, 201, 1500, 29, 131, 111, 210, 600, 202,
+        103, 601, 132, 112, 203, 631, 212, 610, 632, 620, 621, 200, 602, 0, 122, 222, 133, 603,
+        211, 300, 221, 1, 2, 611, 232, 230, 3, 231, 612, 310, 233, 220, 4, 5, 633, 6, 7, 622, 320,
+        8, 330, 10, 12,
+    ),
+)
+SCATTER_PLANS = (
+    (
+        6, 7, 10, 11, 13, 14, 12, 1221, 730, 15, 16, 1231, 17, 1211, 18, 720, 19, 20, 1212, 830,
+        1232, 21, 700, 1201, 1202, 930, 1310, 1031, 1233, 800, 1222, 820, 22, 30, 710, 1203, 900,
+        1001, 920, 1021, 1002, 31, 1032, 810, 1300, 32, 1033, 1320, 1022, 910, 1410, 1011, 1330,
+        1430, 1400, 33, 1012, 1003, 1110, 1420, 1130, 1100, 1120,
+    ),
+    (
+        9, 11, 1231, 730, 14, 15, 16, 830, 13, 720, 1221, 18, 19, 17, 710, 1211, 930, 1031, 820,
+        20, 21, 22, 23, 24, 1212, 25, 810, 700, 920, 1201, 1202, 26, 1222, 1021, 1232, 910, 1310,
+        1011, 30, 1233, 1032, 800, 1022, 31, 1320, 32, 1012, 1420, 900, 1203, 1033, 1001, 1410,
+        1130, 1002, 33, 1300, 1110, 1330, 1120, 1003, 1400, 1100, 1430,
+    ),
+)
+
+
+def body(images, text, enc_mats, enc_vecs, dec_mats, dec_vecs, tissue, text_len, enc_cot, dec_cot):
+    shards = lax.axis_size("dp")
+    img_count, slots = tissue.shape
+    words = text.shape[0] // img_count
+    fits = (
+        shards == 16
+        and img_count == 2
+        and slots <= BLOCK == 256
+        and img_count * words == BLOCK
+        and enc_mats.shape[0] % LINES == 0
+        and dec_mats.shape[0] % LINES == 0
+        and enc_vecs.shape[0] % VEC_UNIT == 0
+        and dec_vecs.shape[0] % VEC_UNIT == 0
+    )
+    run = body_fast if fits else body_plain
+    return run(
+        images, text, enc_mats, enc_vecs, dec_mats, dec_vecs, tissue, text_len, enc_cot, dec_cot
+    )
+
+
 def solution(mesh):
     placed = (
         P("dp", None),

time: 1360 us -> 318 us (0.23)
  waiting for transfers between devices: 760 us -> 0 us
  Pallas kernels: 0 us -> 311 us
  blocking collectives: 158 us -> 0 us
  local copies, waits for them, and re-layouts: 154 us -> 2.76 us
  other arithmetic: 141 us -> 0 us
  matrix products: 98.4 us -> 0 us
  loops' own time: 22.5 us -> 0 us
  between operations: 15.6 us -> 0.89 us
    reduce_scatter x1 -> x0, waiting for transfers between devices: 534 us -> none  [body(): lax.psum_scatter(total_mats, 'dp', scatter_dimension=0, tiled=True)]
    pallas_call x0 -> x2, Pallas kernels: none -> 311 us  [the longest x1 305 us: body_fast(): pl.pallas_call(functools.partial(fused_kernel, depth, sizes, pers, wide,...]
    unnamed x2 -> x0, blocking collectives: 156 us -> none
    all_gather x1 -> x0, waiting for transfers between devices: 135 us -> none  [body(): lax.all_gather(own_mats, 'dp', axis=0, tiled=True)]
    dot_general x42 -> x0, matrix products: 91.1 us -> none  [the longest x2 13.7 us: mlp_block(): jnp.einsum('bsf,fd->bsd', hidden, w_out, preferred_element_type=jnp.float32)]
    ppermute x4 -> x0, waiting for transfers between devices: 90.8 us -> none  [shifted(): return lax.ppermute(block, axis, route)]
    slice x40 -> x0, local copies, waits for them, and re-layouts: 55.5 us -> none  [the longest x4 26.7 us: enc_view(): weights[0].reshape(shards, dec_rows, D)[:, :enc_rows]]
    concatenate x3 -> x0, other arithmetic: 54.6 us -> none  [the longest x2 53.5 us: encode_back(): grad_mats = jnp.concatenate(mats_self + mats_mlp, axis=0)]
  transfers between devices with their start and end apart: 7 -> 0, of which waited for: 5 -> 0; matrix products, arithmetic and copies ran while one was open for 1% -> 0% of each run, Pallas kernels for 0% -> 0%
where the time goes in v1:
time: 318 us; the launch traced here: 315 us
  Pallas kernels  311 us (98%)
    pallas_call x1, Pallas kernels, body_fast(): pl.pallas_call(functools.partial(fused_kernel, depth, sizes, pers, wide,...  305 us
    pallas_call x1, Pallas kernels, body_fast(): pl.pallas_call(functools.partial(finish_kernel, slots), grid=(FINISH_STEP...  6.56 us

profile of v1, /device:TPU:0, one launch (start us, length us, event | category | flops | bytes accessed | tf_op | source)
XLA Modules:
  0.0 315.1 jit_solution(16574989686801775481)
XLA Ops:
  0.6 0.8 reshape.28
  1.4 0.6 pad.8.enc_tile
  2.0 0.8 reshape.29
  2.8 0.6 pad.9.dec_tile
  3.4 304.9 %blocks_and_grads.1 = (bf16[512,768]{1,0:T(8,128)(2,1)}, bf16[256,768]{1,0:T(8,128)(2,1)}, bf16[512,768]{1,0:T(8,128)(2,1)}, bf16[256,768]{1,0:T(8,128)(2,1)}, b...) custom-call(bf16[392,768]{1,0:T(8,128)(2,1)} %images_in.1, ...), custom_call_target="tpu_custom_call" | custom-call | tf_op jit(solution)/shard_map/blocks_and_grads/pallas_call | solution.py:1969
  308.3 6.6 %finish_outputs.1 = (bf16[392,768]{1,0:T(8,128)(2,1)}, bf16[256,768]{1,0:T(8,128)(2,1)}, f32[392,768]{1,0:T(8,128)}, f32[256,768]{1,0:T(8,128)}, f32[576,768]{1,...) custom-call(bf16[512,768]{1,0:T(8,128)(2,1)} %get-tuple-element.24.encoded, ...), custom_call_target="tpu_custom_call" | custom-call | tf_op jit(solution)/shard_map/finish_outputs/pallas_call | solution.py:2051

commit v2 on v1

--- a/solution.py
+++ b/solution.py
@@ -1044,14 +1044,19 @@
 
 
 class Compute:
-    def __init__(self, w, vrows, gvec, red):
+    def __init__(self, w, vrows, gvec, red, eye):
         self.w = w
+        self.eye = eye
         self.vrows = vrows
         self.gvec = gvec
         self.red = red
 
     def vec(self, index):
         return self.vrows[pl.ds(index, 1), :]
+
+    def turned(self, values):
+        size = values.shape[1]
+        return dot_nt(self.eye[pl.ds(0, size), pl.ds(0, size)], values).astype(BF16)
 
     def norm(self, src, src_row, dst, dst_row, rows, gain, shift, unit, unit_row, rate, rate_row):
         scale_vec, shift_vec = self.vec(gain), self.vec(shift)
@@ -1189,7 +1194,7 @@
         @pl.loop(0, PAIRS, unroll=ATTEND_UNROLL)
         def _(pair):
             keys = k_at(pair)[...]
-            values = v_at(pair)[...].T
+            values = self.turned(v_at(pair)[...])
             mixed = []
             for half, queries in enumerate(self.halves(q_at(pair)[...], 0.125)):
                 scores = jnp.where(allowed, dot_nt(keys, queries), -1000000000.0)
@@ -1198,12 +1203,12 @@
                 probs = (expd * rate).astype(BF16)
                 p_at(pair, half)[...] = probs
                 mixed.append(dot_nn(values, probs)[half * HEAD : (half + 1) * HEAD])
-            o_at(pair)[...] = jnp.concatenate(mixed, axis=0).T.astype(BF16)
+            o_at(pair)[...] = self.turned(jnp.concatenate(mixed, axis=0).astype(BF16))
 
     def attend_back(self, q_at, k_at, v_at, p_at, do_at):
         @pl.loop(0, PAIRS, unroll=ATTEND_UNROLL)
         def _(pair):
-            keys = k_at(pair)[...].T
+            keys = self.turned(k_at(pair)[...])
             values = v_at(pair)[...]
             grad_q, grad_k, grad_v = [], 0.0, 0.0
             both = zip(self.halves(q_at(pair)[...], 0.125), self.halves(do_at(pair)[...]))
@@ -1216,7 +1221,8 @@
                 grad_q.append(dot_nn(keys, grad_scores)[half * HEAD : (half + 1) * HEAD])
                 grad_k = grad_k + dot_nn(grad_scores, queries)
                 grad_v = grad_v + dot_nn(low, grads)
-            q_at(pair)[...] = (jnp.concatenate(grad_q, axis=0) * 0.125).T.astype(BF16)
+            grad_q = jnp.concatenate(grad_q, axis=0) * 0.125
+            q_at(pair)[...] = self.turned(grad_q.astype(BF16))
             k_at(pair)[...] = grad_k.astype(BF16)
             v_at(pair)[...] = grad_v.astype(BF16)
 
@@ -1278,6 +1284,7 @@
     vland,
     vout,
     red,
+    eye,
     load_sems,
     ag_send,
     ag_recv,
@@ -1300,7 +1307,7 @@
     section = place.section
     image_rows, text_rows = xin.shape[0], text_in.shape[0]
     images, used = tissue.shape
-    comp = Compute(w, vrows, gvec, red)
+    comp = Compute(w, vrows, gvec, red, eye)
     cuts = [split_rows(rows, LATE) for rows in sizes]
 
     def load(index, src, dst, waiting=False):
@@ -1449,6 +1456,9 @@
         )
 
     def start_stage(which):
+        eye[...] = jnp.where(
+            iota((BLOCK, BLOCK), 0) == iota((BLOCK, BLOCK), 1), 1.0, 0.0
+        ).astype(BF16)
         got_vecs()
         vrows[...] = vec_gathered(tiles, pers[which])
         gvec[...] = jnp.zeros_like(gvec)
@@ -2007,6 +2017,7 @@
             pltpu.VMEM((1 + depth, VEC_ROWS, D), F32),
             pltpu.VMEM((VEC_ROWS, 128), F32),
             pltpu.VMEM((2, 8, D), F32),
+            low_buffer(BLOCK, BLOCK),
             dma((6,)),
             dma((4, shards, 4)),
             dma((4, shards)),

time: 318 us -> 319 us (level)
  no operation moved by 1% of the time
where the time goes in v2:
time: 319 us; the launch traced here: 316 us
  Pallas kernels  312 us (98%)
    pallas_call x1, Pallas kernels, body_fast(): pl.pallas_call(functools.partial(fused_kernel, depth, sizes, pers, wide,...  305 us
    pallas_call x1, Pallas kernels, body_fast(): pl.pallas_call(functools.partial(finish_kernel, slots), grid=(FINISH_STEP...  6.56 us

profile of v2, /device:TPU:0, one launch (start us, length us, event | category | flops | bytes accessed | tf_op | source)
XLA Modules:
  0.0 315.7 jit_solution(13962362676766789144)
XLA Ops:
  0.6 0.8 reshape.28
  1.4 0.6 pad.8.enc_tile
  2.0 0.8 reshape.29
  2.8 0.6 pad.9.dec_tile
  3.4 305.5 %blocks_and_grads.1 = (bf16[512,768]{1,0:T(8,128)(2,1)}, bf16[256,768]{1,0:T(8,128)(2,1)}, bf16[512,768]{1,0:T(8,128)(2,1)}, bf16[256,768]{1,0:T(8,128)(2,1)}, b...) custom-call(bf16[392,768]{1,0:T(8,128)(2,1)} %images_in.1, ...), custom_call_target="tpu_custom_call" | custom-call | tf_op jit(solution)/shard_map/blocks_and_grads/pallas_call | solution.py:1979
  308.9 6.6 %finish_outputs.1 = (bf16[392,768]{1,0:T(8,128)(2,1)}, bf16[256,768]{1,0:T(8,128)(2,1)}, f32[392,768]{1,0:T(8,128)}, f32[256,768]{1,0:T(8,128)}, f32[576,768]{1,...) custom-call(bf16[512,768]{1,0:T(8,128)(2,1)} %get-tuple-element.24.encoded, ...), custom_call_target="tpu_custom_call" | custom-call | tf_op jit(solution)/shard_map/finish_outputs/pallas_call | solution.py:2062

commit v3 on v1

--- a/solution.py
+++ b/solution.py
@@ -686,6 +686,48 @@
             self.arrived(cls, place.pair(cls == 0, plane, a, 1 - b))
             self.arrived(cls, place.pair(cls == 0, plane, 1 - a, 1 - b))
 
+    def drain(self):
+        place = self.place
+        z, last = place.z, self.depth - 1
+
+        def left(cls, shard, way):
+            piece = self.piece(cls, shard)
+            pltpu.make_async_remote_copy(
+                src_ref=piece,
+                dst_ref=piece,
+                send_sem=self.send_sems.at[cls, shard, way],
+                recv_sem=self.recv_sems.at[cls, shard],
+                device_id=(place.section, place.me),
+                device_id_type=MESH,
+            ).wait_send()
+
+        for cls in (0, 1) + self.late:
+            first_x = cls in (0, 2)
+            a, b = place.own(first_x)
+            early = cls < 2
+
+            def in_plane(plane):
+                own = place.shard(plane, place.y, place.x)
+                left(cls, own, 2)
+                left(cls, own, 3)
+                left(cls, place.pair(first_x, plane, 1 - a, b), 3)
+
+            def along(plane, way):
+                if early:
+                    left(cls, place.shard(plane, place.y, place.x), way)
+                else:
+                    pl.loop(0, 4)(lambda index: left(cls, plane * 4 + index, way))
+
+            @pl.loop(0, self.depth)
+            def _(plane):
+                if early:
+                    in_plane(plane)
+                pl.when((z >= plane) & (z < last))(lambda: along(plane, 0))
+                pl.when((z <= plane) & (z > 0))(lambda: along(plane, 1))
+
+            if not early:
+                in_plane(z)
+
     def X(self):
         if not self.copies.waiting:
             self.gate()
@@ -794,6 +836,38 @@
             self.cuts[cls][1],
         )
 
+    def drain(self):
+        z, depth = self.place.z, self.depth
+
+        def left(cls, slot):
+            piece = self.slot_ref(cls, slot)
+            pltpu.make_async_remote_copy(
+                src_ref=piece,
+                dst_ref=piece,
+                send_sem=self.send_sems.at[cls, slot],
+                recv_sem=self.recv_sems.at[cls, slot],
+                device_id=(self.place.section, self.place.me),
+                device_id_type=MESH,
+            ).wait_send()
+
+        for cls in (0, 1):
+            pl.loop(0, 3 * depth)(lambda slot: left(cls, slot))
+
+            @pl.loop(0, depth)
+            def _(plane):
+                pl.when(z == plane + 1)(lambda: left(cls, 4 * depth))
+                pl.when((z > plane + 1) | (z < plane))(lambda: left(cls, 3 * depth + plane))
+
+        for cls in self.late:
+
+            @pl.loop(0, 4 * depth)
+            def _(index):
+                plane, piece = lax.div(index, 4), lax.rem(index, 4)
+                pl.when(z == plane + 1)(lambda: left(cls, 4 * depth + piece))
+                pl.when((z > plane + 1) | (z < plane))(lambda: left(cls, index))
+
+            pl.loop(0, 3)(lambda hop: left(cls, 4 * depth + 4 + hop))
+
     def A(self, plane):
         place = self.place
         for cls in (0, 1):
@@ -914,19 +988,11 @@
 STEPS = "CLGHMNTABPZEQRSX"
 
 
-LAG = 14
-
-
-class Plan:
-    def __init__(self, steps, copies, sent, stages):
-        self.steps = steps
-        self.copies = copies
-        self.sent = sent
-        self.stages = stages
-        self.open = []
-
-    @staticmethod
-    def act(copies, step):
+def run_plan(steps, copies, stages):
+    for step in steps:
+        if step < 100:
+            stages[step]()
+            continue
         kind, plane, hop = step // 100, step // 10 % 10, step % 10
         act = getattr(copies, STEPS[kind])
         if STEPS[kind] in "LGTZQ":
@@ -935,21 +1001,6 @@
             act()
         else:
             act(plane)
-
-    def run(self):
-        for step in self.steps:
-            if step < 100:
-                self.stages[step]()
-                continue
-            self.act(self.copies, step)
-            self.open.append(step)
-            if len(self.open) > LAG:
-                self.act(self.sent, self.open.pop(0))
-
-    def flush(self):
-        for step in self.open:
-            self.act(self.sent, step)
-        self.open.clear()
 
 
 BLOCK = 256
@@ -1474,19 +1525,16 @@
 
     def section_program(which, make):
         stages = sum_stages(which)
-        gathering = Plan(GATHER_PLANS[which], gather(which), gather(which, True), stages)
-        scattering = Plan(SCATTER_PLANS[which], scatter(which), scatter(which, True), stages)
-
         def gathered():
-            gathering.flush()
+            gather(which).drain()
             give_vecs(True)
 
         made, last = make(gathered)
         stages.update(made)
         load_own(which, True)
-        gathering.run()
-        scattering.run()
-        scattering.flush()
+        run_plan(GATHER_PLANS[which], gather(which), stages)
+        run_plan(SCATTER_PLANS[which], scatter(which), stages)
+        scatter(which).drain()
         for cls in range(4):
             give_class(True, which, cls)
         give(True, 6, vout, (enc_v, dec_v)[which])

time: 318 us -> 318 us (level)
  no operation moved by 1% of the time
where the time goes in v3:
time: 318 us; the launch traced here: 316 us
  Pallas kernels  312 us (98%)
    pallas_call x1, Pallas kernels, body_fast(): pl.pallas_call(functools.partial(fused_kernel, depth, sizes, pers, wide,...  305 us
    pallas_call x1, Pallas kernels, body_fast(): pl.pallas_call(functools.partial(finish_kernel, slots), grid=(FINISH_STEP...  6.57 us

profile of v3, /device:TPU:0, one launch (start us, length us, event | category | flops | bytes accessed | tf_op | source)
XLA Modules:
  0.0 315.7 jit_solution(4046563533917098885)
XLA Ops:
  0.6 0.8 reshape.28
  1.4 0.6 pad.8.enc_tile
  2.0 0.8 reshape.29
  2.8 0.6 pad.9.dec_tile
  3.4 305.5 %blocks_and_grads.1 = (bf16[512,768]{1,0:T(8,128)(2,1)}, bf16[256,768]{1,0:T(8,128)(2,1)}, bf16[512,768]{1,0:T(8,128)(2,1)}, bf16[256,768]{1,0:T(8,128)(2,1)}, b...) custom-call(bf16[392,768]{1,0:T(8,128)(2,1)} %images_in.1, ...), custom_call_target="tpu_custom_call" | custom-call | tf_op jit(solution)/shard_map/blocks_and_grads/pallas_call | solution.py:2017
  308.9 6.6 %finish_outputs.1 = (bf16[392,768]{1,0:T(8,128)(2,1)}, bf16[256,768]{1,0:T(8,128)(2,1)}, f32[392,768]{1,0:T(8,128)}, f32[256,768]{1,0:T(8,128)}, f32[576,768]{1,...) custom-call(bf16[512,768]{1,0:T(8,128)(2,1)} %get-tuple-element.24.encoded, ...), custom_call_target="tpu_custom_call" | custom-call | tf_op jit(solution)/shard_map/finish_outputs/pallas_call | solution.py:2099
